TPU v7x, 32 devices: a whole 2x2x4 slice. The times are simulated.
32 devices in a mesh: seq: 8 (over z, y), grp: 4 (over x, core).
Axes of the slice: x: 2, y: 2, z: 4, core: 2. Of those that a mesh axis runs over, the one named last changes fastest.
Arguments:
- frames_in: float32 [4, 1024, 512], P('grp', 'seq'), may hold values from -6 to 6
- cotangent: float32 [4, 1024, 512], P('grp', 'seq'), may hold values from -6 to 6
- lengths: int32 [4, 4], P('grp'), may hold values from 1 to 1024, as said below
- rate_flags: int32 [4, 4], P('grp'), may hold values 0 or 1
- owner_list: int32 [48, 1], replicated, may hold values from 0 to 3; in each aligned block of 48 rows (0 to 47, 48 to 95, ...) at most 16 rows name the same one
- master: float32 [64, 262144], P('grp', 'seq'), may hold values from -0.25 to 0.25
- moment_one: float32 [64, 262144], P('grp', 'seq'), may hold values from -6 to 6
- moment_two: float32 [64, 262144], P('grp', 'seq'), may hold values from 0.16384 to 0.65536
- average: float32 [64, 262144], P('grp', 'seq'), may hold values from -0.25 to 0.25
- small_params: float32 [2, 23, 512], replicated
- small_moment_one: float32 [2, 23, 512], replicated, may hold values from -20 to 20
- small_moment_two: float32 [2, 23, 512], replicated, may hold values from 0.8192 to 3.2768
- small_average: float32 [2, 23, 512], replicated
Outputs:
- output: float32 [4, 1024, 512], P('grp', 'seq')
- grad_in: float32 [4, 1024, 512], P('grp', 'seq')
- new_master: float32 [64, 262144], P('grp', 'seq')
- master_copy: bfloat16 [64, 262144], P('grp', 'seq')
- new_moment_one: float32 [64, 262144], P('grp', 'seq')
- new_moment_two: float32 [64, 262144], P('grp', 'seq')
- new_average: float32 [64, 262144], P('grp', 'seq')
- new_small: float32 [2, 23, 512], replicated
- new_small_one: float32 [2, 23, 512], replicated
- new_small_two: float32 [2, 23, 512], replicated
- new_small_average: float32 [2, 23, 512], replicated
Inputs may be any that keep to these rules, and one draw needn't show every extreme that they name: `lengths`: each row sums to 1024. In each row one item, at a place drawn from the seed, starts within the first 128 frames and ends within the last 128; every other item has at most 32 frames. `owner_list`: each owner holds at most 16 blocks, and some owner holds exactly 16.
All inputs are finite; a program needn't handle non-finite values. No bound on the sum of `rate_flags` on one device may be relied on, other than what follows from the above.
Results may differ from a plain program's by a relative error of at most 0.001.
Values sent between devices are 32-bit elements; how exact they have to be, the bound alone decides.
A program may use at most 384 MiB of HBM per device.

v0:
```python
from functools import partial
import math

import jax
import jax.numpy as jnp
from jax import lax
from jax.sharding import PartitionSpec as P

HEADS = 8
KERNEL = 9
NB = 128
L = 2
CAP = 16
STEP = 10


PRECISION_HIGH = lax.Precision.HIGHEST
EPS_NORM = 1e-05
BETA_ONE = 0.9
BETA_TWO = 0.999
ADAM_EPS = 1e-08
RATE_MATRIX = 0.03
RATE_SMALL = 0.1
DECAY_WEIGHT = 0.01
AVERAGE_KEEP = 0.99


def with_halo(block, sides, width):
    for axis, dim in sides:
        count = lax.axis_size(axis)
        forward = [(i, i + 1) for i in range(count - 1)]
        backward = [(target, source) for source, target in forward]
        low = lax.ppermute(
            lax.slice_in_dim(block, block.shape[dim] - width, None, axis=dim), axis, forward
        )
        high = lax.ppermute(lax.slice_in_dim(block, 0, width, axis=dim), axis, backward)
        block = jnp.concatenate([low, block, high], axis=dim)
    return block


def product(left, right):
    return jnp.dot(left, right, precision=PRECISION_HIGH)


def layer_norm(values, norm_gain, norm_shift):
    center = values - jnp.mean(values, axis=-1, keepdims=True)
    spread = jnp.mean(center * center, axis=-1, keepdims=True)
    return center * lax.rsqrt(spread + EPS_NORM) * norm_gain + norm_shift


def widen_blocks(blocks):
    return jnp.transpose(blocks, (1, 0, 2)).reshape(blocks.shape[1], -1)


def feed_forward(values, blocks, norm_gain, norm_shift):
    normed = layer_norm(values, norm_gain, norm_shift)
    hidden = jax.nn.silu(product(normed, widen_blocks(blocks[0:4])))
    return 0.5 * product(hidden, blocks[4:8].reshape(-1, values.shape[-1]))


def rel_table(bucket_count, hidden_width):
    offset = (jnp.arange(bucket_count, dtype=jnp.int32) - bucket_count // 2).astype(jnp.float32)[
        :, None
    ]
    column = jnp.arange(hidden_width, dtype=jnp.int32)
    frequency = jnp.exp(
        -math.log(10000.0) * (2 * (column // 2)).astype(jnp.float32) / hidden_width
    )[None, :]
    angles = offset * frequency
    return jnp.where(column[None, :] % 2 == 0, jnp.sin(angles), jnp.cos(angles))


def attention_inputs(values, w_query, w_key, w_value, w_pos, norm_gain, norm_shift, bias_u, bias_v):
    normed = layer_norm(values, norm_gain, norm_shift)
    queries = product(normed, w_query)
    pos_table = product(rel_table(NB, values.shape[-1]), w_pos)
    return (
        queries + bias_u,
        queries + bias_v,
        pos_table,
        product(normed, w_key),
        product(normed, w_value),
    )


def conv_inputs(values, w_value, w_gate, norm_gain, norm_shift):
    normed = layer_norm(values, norm_gain, norm_shift)
    return product(normed, w_value) * jax.nn.sigmoid(product(normed, w_gate))


def conv_outputs(extended, kernel_rows, w_out, norm_gain, norm_shift, item_mask):
    row_count = extended.shape[0] - KERNEL + 1
    mixed_rows = jnp.zeros((row_count, extended.shape[1]), jnp.float32)
    for tap_index in range(KERNEL):
        mixed_rows = (
            mixed_rows
            + extended[tap_index : tap_index + row_count]
            * item_mask[tap_index][:, None]
            * kernel_rows[tap_index]
        )
    normed = layer_norm(mixed_rows, norm_gain, norm_shift)
    return product(jax.nn.silu(normed), w_out)


def frame_info(frame_index, lengths_row, flags_row):
    item_ends = jnp.cumsum(lengths_row)
    item_starts = item_ends - lengths_row
    inside = (frame_index[:, None] >= item_starts[None, :]) & (
        frame_index[:, None] < item_ends[None, :]
    )
    numbers = jnp.arange(lengths_row.shape[0], dtype=jnp.int32)
    frame_items = jnp.sum(jnp.where(inside, numbers[None, :] + 1, 0), axis=1) - 1
    first_frame = jnp.sum(jnp.where(inside, item_starts[None, :], 0), axis=1)
    stride = jnp.sum(jnp.where(inside, 1 + flags_row[None, :], 0), axis=1)
    return (frame_items, (frame_index - first_frame) * stride)


def slot_index(owner_list):
    owners = owner_list[:, 0]
    numbers = jnp.arange(owners.shape[0], dtype=jnp.int32)
    earlier = (owners[None, :] == owners[:, None]) & (numbers[None, :] < numbers[:, None])
    owner_rank = jnp.sum(earlier.astype(jnp.int32), axis=1)
    return owners * CAP + owner_rank


def adam_step(attention_weights, first_moment, second_moment, gradient, step_rate, decay_rate):
    first_moment = BETA_ONE * first_moment + (1.0 - BETA_ONE) * gradient
    second_moment = BETA_TWO * second_moment + (1.0 - BETA_TWO) * gradient * gradient
    fixed_one = 1.0 - BETA_ONE**STEP
    fixed_two = 1.0 - BETA_TWO**STEP
    direction = first_moment / fixed_one / (jnp.sqrt(second_moment / fixed_two) + ADAM_EPS)
    return (
        attention_weights - step_rate * (direction + decay_rate * attention_weights),
        first_moment,
        second_moment,
    )


def attention_core(q_u, q_v, pos_table, key_rows, value_rows, item_q, stride_q, row_start, item_k):
    row_count, hidden_width = q_u.shape
    head_size = hidden_width // HEADS
    bucket_count = pos_table.shape[0]
    half_buckets = bucket_count // 2
    rows_per_block = 4 * row_count
    block_count = key_rows.shape[0] // rows_per_block
    score_scale = 1.0 / math.sqrt(head_size)
    query_with_bias = q_u.reshape(row_count, HEADS, head_size)
    query_pos = jnp.einsum(
        "nhd,bhd->hnb",
        q_v.reshape(row_count, HEADS, head_size),
        pos_table.reshape(bucket_count, HEADS, head_size),
        precision=PRECISION_HIGH,
    )
    bucket_numbers = jnp.arange(bucket_count, dtype=jnp.int32)
    doubled = (
        jnp.clip(2 * (bucket_numbers - half_buckets), -half_buckets, half_buckets - 1)
        + half_buckets
    )
    select = (bucket_numbers[:, None] == doubled[None, :]).astype(jnp.float32)
    pos_doubled = jnp.einsum("hqb,bt->hqt", query_pos, select, precision=PRECISION_HIGH)
    near = jnp.where(stride_q[None, :, None] == 2, pos_doubled, query_pos)
    band_width = row_count + bucket_count
    shifted = jnp.pad(near, ((0, 0), (0, 0), (row_count - 1, 1)))
    flat = jnp.pad(shifted.reshape(HEADS, row_count * band_width), ((0, 0), (0, row_count)))
    band = flat.reshape(HEADS, row_count, band_width + 1)[:, :, :band_width][:, :, ::-1]
    band = jnp.pad(band, ((0, 0), (0, 0), (rows_per_block, rows_per_block)))
    last_bucket = query_pos[:, :, bucket_count - 1 : bucket_count]
    first_bucket = query_pos[:, :, 0:1]
    local_rows = jnp.arange(row_count, dtype=jnp.int32)
    query_rows = row_start + local_rows
    key_blocks = key_rows.reshape(block_count, rows_per_block, HEADS, head_size)
    value_blocks = value_rows.reshape(block_count, rows_per_block, HEADS, head_size)
    item_blocks = item_k.reshape(block_count, rows_per_block)
    block_starts = jnp.arange(block_count, dtype=jnp.int32) * rows_per_block

    def visit(carried, inputs):
        row_top, row_total, summed = carried
        block_of_keys, block_of_values, item_block, block_start = inputs
        attention_scores = jnp.einsum(
            "qbp,cbp->bqc", query_with_bias, block_of_keys, precision=PRECISION_HIGH
        )
        key_index = block_start + jnp.arange(rows_per_block, dtype=jnp.int32)
        band_block = lax.dynamic_slice_in_dim(
            band, block_start - row_start + half_buckets + rows_per_block, rows_per_block, 2
        )
        place = key_index[None, :] - row_start + half_buckets
        inband = (place >= local_rows[:, None] + 1) & (place <= local_rows[:, None] + bucket_count)
        far = jnp.where((key_index[None, :] < query_rows[:, None])[None], last_bucket, first_bucket)
        attention_scores = attention_scores + jnp.where(inband[None], band_block, far)
        attention_scores = attention_scores * score_scale
        same_item = (item_q[:, None] == item_block[None, :])[None]
        attention_scores = jnp.where(same_item, attention_scores, -1e30)
        new_top = jnp.maximum(row_top, jnp.max(attention_scores, axis=-1))
        factor = jnp.exp(row_top - new_top)
        attention_weights = jnp.where(
            same_item, jnp.exp(attention_scores - new_top[..., None]), 0.0
        )
        row_total = row_total * factor + jnp.sum(attention_weights, axis=-1)
        summed = summed * factor[..., None] + jnp.einsum(
            "cuq,qcz->cuz", attention_weights, block_of_values, precision=PRECISION_HIGH
        )
        return ((new_top, row_total, summed), None)

    initial = (
        jnp.full((HEADS, row_count), -1e30, jnp.float32),
        jnp.zeros((HEADS, row_count), jnp.float32),
        jnp.zeros((HEADS, row_count, head_size), jnp.float32),
    )
    (row_top, row_total, summed), _ = lax.scan(
        jax.checkpoint(visit), initial, (key_blocks, value_blocks, item_blocks, block_starts)
    )
    context = summed / row_total[..., None]
    return jnp.transpose(context, (1, 0, 2)).reshape(row_count, hidden_width)


def on_device(
    frames_in,
    cotangent,
    lengths,
    rate_flags,
    owner_list,
    master,
    moment_one,
    moment_two,
    average,
    small_params,
    small_moment_one,
    small_moment_two,
    small_average,
):
    local_rows = frames_in.shape[1]
    hidden_width = frames_in.shape[2]
    stream_rows = local_rows * lax.axis_size("seq")
    first_row = lax.axis_index("seq") * local_rows
    half_width = (KERNEL - 1) // 2
    lengths_row = lengths[0]
    flags_row = rate_flags[0]
    own_index = first_row + jnp.arange(local_rows, dtype=jnp.int32)
    own_items, own_places = frame_info(own_index, lengths_row, flags_row)
    item_numbers = jnp.arange(lengths_row.shape[0], dtype=jnp.int32)
    own_stride = 1 + jnp.sum(
        jnp.where(own_items[:, None] == item_numbers[None, :], flags_row[None, :], 0), axis=1
    )
    key_items, key_places = frame_info(
        jnp.arange(stream_rows, dtype=jnp.int32), lengths_row, flags_row
    )
    rim_index = first_row - half_width + jnp.arange(local_rows + 2 * half_width, dtype=jnp.int32)
    rim_items, _ = frame_info(rim_index, lengths_row, flags_row)
    item_mask = jnp.stack(
        [
            (rim_items[tap_index : tap_index + local_rows] == own_items).astype(jnp.float32)
            for tap_index in range(KERNEL)
        ]
    )
    core = partial(
        attention_core, item_q=own_items, stride_q=own_stride, row_start=first_row, item_k=key_items
    )
    conv_local = partial(conv_outputs, item_mask=item_mask)
    slot_of = slot_index(owner_list)
    columns = lax.all_gather(master, "seq", axis=1, tiled=True)
    slot_rows = lax.all_gather(columns, "grp", axis=0, tiled=True)
    blocks_all = slot_rows[slot_of].reshape(-1, hidden_width, hidden_width)
    values = frames_in[0]
    saved = []
    for layer_index in range(L):
        blocks = blocks_all[24 * layer_index : 24 * layer_index + 24]
        rows_small = small_params[layer_index]
        start_values = values
        after_ffn = values + feed_forward(values, blocks[0:8], rows_small[0], rows_small[1])
        q_u, q_v, pos_table, key_rows, value_rows = attention_inputs(
            after_ffn,
            blocks[8],
            blocks[9],
            blocks[10],
            blocks[12],
            rows_small[2],
            rows_small[3],
            rows_small[12 + KERNEL],
            rows_small[13 + KERNEL],
        )
        all_keys, all_values = (
            lax.all_gather(key_rows, "seq", axis=0, tiled=True),
            lax.all_gather(value_rows, "seq", axis=0, tiled=True),
        )
        context = core(q_u, q_v, pos_table, all_keys, all_values)
        after_attention = after_ffn + product(context, blocks[11])
        glu_rows = conv_inputs(
            after_attention, blocks[13], blocks[14], rows_small[4], rows_small[5]
        )
        extended = with_halo(glu_rows, (("seq", 0),), half_width)
        after_conv = after_attention + conv_local(
            extended, rows_small[12 : 12 + KERNEL], blocks[15], rows_small[6], rows_small[7]
        )
        after_second = after_conv + feed_forward(
            after_conv, blocks[16:24], rows_small[8], rows_small[9]
        )
        values = layer_norm(after_second, rows_small[10], rows_small[11])
        kept = (all_keys, all_values)
        saved.append(
            (
                start_values,
                after_ffn,
                after_attention,
                extended,
                after_conv,
                after_second,
                context,
                kept,
            )
        )
    grad_values = cotangent[0]
    layer_blocks = [None] * L
    layer_rows = [None] * L
    for layer_index in reversed(range(L)):
        blocks = blocks_all[24 * layer_index : 24 * layer_index + 24]
        rows_small = small_params[layer_index]
        (
            start_values,
            after_ffn,
            after_attention,
            extended,
            after_conv,
            after_second,
            context,
            kept,
        ) = saved[layer_index]
        _, pull_back = jax.vjp(layer_norm, after_second, rows_small[10], rows_small[11])
        grad_second, final_gain, final_shift = pull_back(grad_values)
        _, pull_back = jax.vjp(
            feed_forward, after_conv, blocks[16:24], rows_small[8], rows_small[9]
        )
        step_values, second_blocks, second_gain, second_shift = pull_back(grad_second)
        grad_conv = grad_second + step_values
        _, pull_back = jax.vjp(
            conv_local,
            extended,
            rows_small[12 : 12 + KERNEL],
            blocks[15],
            rows_small[6],
            rows_small[7],
        )
        grad_extended, kernel_grads, conv_out_grad, inner_gain, inner_shift = pull_back(grad_conv)
        rim_pair = jnp.concatenate(
            [grad_extended[:half_width], grad_extended[-half_width:]], axis=0
        )
        rims = with_halo(rim_pair, (("seq", 0),), half_width)
        grad_glu = grad_extended[half_width:-half_width]
        grad_glu = (
            grad_glu.at[:half_width].add(rims[:half_width]).at[-half_width:].add(rims[-half_width:])
        )
        _, pull_back = jax.vjp(
            conv_inputs, after_attention, blocks[13], blocks[14], rows_small[4], rows_small[5]
        )
        step_values, conv_value_grad, conv_gate_grad, conv_gain, conv_shift = pull_back(grad_glu)
        grad_attention = grad_conv + step_values
        output_proj_grad = product(context.T, grad_attention)
        grad_context = product(grad_attention, blocks[11].T)
        attention_parts, pull_inputs = jax.vjp(
            attention_inputs,
            after_ffn,
            blocks[8],
            blocks[9],
            blocks[10],
            blocks[12],
            rows_small[2],
            rows_small[3],
            rows_small[12 + KERNEL],
            rows_small[13 + KERNEL],
        )
        q_u, q_v, pos_table, key_rows, value_rows = attention_parts
        all_keys, all_values = kept
        _, pull_core = jax.vjp(core, q_u, q_v, pos_table, all_keys, all_values)
        grad_qu, grad_qv, grad_table, grad_keys_all, grad_values_all = pull_core(grad_context)
        grad_keys, grad_vals = (
            lax.psum_scatter(grad_keys_all, "seq", scatter_dimension=0, tiled=True),
            lax.psum_scatter(grad_values_all, "seq", scatter_dimension=0, tiled=True),
        )
        (
            step_values,
            query_grad,
            key_grad,
            value_grad,
            pos_grad,
            attention_gain,
            attention_shift,
            bias_u_grad,
            bias_v_grad,
        ) = pull_inputs((grad_qu, grad_qv, grad_table, grad_keys, grad_vals))
        grad_ffn = grad_attention + step_values
        _, pull_back = jax.vjp(
            feed_forward, start_values, blocks[0:8], rows_small[0], rows_small[1]
        )
        step_values, first_blocks, first_gain, first_shift = pull_back(grad_ffn)
        grad_values = grad_ffn + step_values
        layer_blocks[layer_index] = jnp.concatenate(
            [
                first_blocks,
                query_grad[None],
                key_grad[None],
                value_grad[None],
                output_proj_grad[None],
                pos_grad[None],
                conv_value_grad[None],
                conv_gate_grad[None],
                conv_out_grad[None],
                second_blocks,
            ],
            axis=0,
        )
        layer_rows[layer_index] = jnp.concatenate(
            [
                jnp.stack(
                    [
                        first_gain,
                        first_shift,
                        attention_gain,
                        attention_shift,
                        conv_gain,
                        conv_shift,
                        inner_gain,
                        inner_shift,
                        second_gain,
                        second_shift,
                        final_gain,
                        final_shift,
                    ]
                ),
                kernel_grads,
                jnp.stack([bias_u_grad, bias_v_grad]),
            ],
            axis=0,
        )
    block_grads = jnp.concatenate(layer_blocks, axis=0).reshape(blocks_all.shape[0], -1)
    slot_total = master.shape[0] * lax.axis_size("grp")
    shares = lax.psum_scatter(block_grads, "seq", scatter_dimension=1, tiled=True)
    share_table = jnp.zeros((slot_total, shares.shape[1]), jnp.float32).at[slot_of].set(shares)
    owned = lax.psum_scatter(share_table, "grp", scatter_dimension=0, tiled=True)
    small_grads = lax.psum(jnp.stack(layer_rows), ("seq", "grp"))
    new_master, new_one, new_two = adam_step(
        master, moment_one, moment_two, owned, RATE_MATRIX, DECAY_WEIGHT
    )
    new_average = AVERAGE_KEEP * average + (1.0 - AVERAGE_KEEP) * new_master
    new_small, new_small_one, new_small_two = adam_step(
        small_params, small_moment_one, small_moment_two, small_grads, RATE_SMALL, 0.0
    )
    new_small_average = AVERAGE_KEEP * small_average + (1.0 - AVERAGE_KEEP) * new_small
    return (
        values[None],
        grad_values[None],
        new_master,
        new_master.astype(jnp.bfloat16),
        new_one,
        new_two,
        new_average,
        new_small,
        new_small_one,
        new_small_two,
        new_small_average,
    )


def solution(mesh):
    in_specs = (
        P("grp", "seq", None),
        P("grp", "seq", None),
        P("grp", None),
        P("grp", None),
        P(),
        P("grp", "seq"),
        P("grp", "seq"),
        P("grp", "seq"),
        P("grp", "seq"),
        P(),
        P(),
        P(),
        P(),
    )
    out_specs = (
        P("grp", "seq", None),
        P("grp", "seq", None),
        P("grp", "seq"),
        P("grp", "seq"),
        P("grp", "seq"),
        P("grp", "seq"),
        P("grp", "seq"),
        P(),
        P(),
        P(),
        P(),
    )
    return jax.shard_map(
        on_device, mesh=mesh, in_specs=in_specs, out_specs=out_specs, check_vma=False
    )
```

profile of v0, /device:TPU:0, one launch (start us, length us, event | category | flops | bytes accessed | tf_op | source)
XLA Modules:
  0.0 3184.0 jit_solution(2124470039051738021)
XLA Ops:
  8.0 232.6 %all-gather.7.cloned.1.call-done = f32[16,262144]{1,0:T(8,128)} async-done(((f32[16,32768]{1,0:T(8,128)}), f32[16,262144]{1,0:T(8,128)}) %all-gather.7.cloned.1.call-update) | async-done | bytes 16777232 | tf_op jit(solution)/shard_map/all_gather | solution.py:260
  244.9 388.1 %all-gather.9.cloned.1.call-done = f32[64,262144]{1,0:T(8,128)} async-done(((f32[16,262144]{1,0:T(8,128)}), f32[64,262144]{1,0:T(8,128)}) %all-gather.9.cloned.1.call-update) | async-done | bytes 67108880 | tf_op jit(solution)/shard_map/all_gather | solution.py:261
  633.0 16.3 mini-gather-slice.5
  649.4 25.4 gather_fusion.2
  674.8 29.5 fusion.434
  704.3 25.4 gather_fusion.1
  729.7 25.6 gather_fusion
  755.3 13.7 constant_dynamic-update-slice_fusion.2
  771.8 8.5 constant_dynamic-update-slice_fusion.1
  782.6 6.0 constant_dynamic-update-slice_fusion
  788.6 88.1 %slice_reduce_fusion.1 = (f32[262144]{0:T(1024)}, f32[262144]{0:T(1024)}, f32[262144]{0:T(1024)}, f32[262144]{0:T(1024)}, f32[262144]{0:T(1024)}, /*index=5*/f32...) fusion(f32[48,262144]{1,0:T(8,128)} %constant_dynamic-update-sl, ...), kind=kLoop, calls=%fused_computation.328 | loop fusion | bytes 35651584 | tf_op jit(solution)/shard_map/slice | solution.py:288
  876.7 34.4 %fusion.435 = (f32[4,262144]{1,0:T(4,128)}, f32[4,262144]{1,0:T(4,128)}, f32[4,262144]{1,0:T(4,128)}, f32[4,262144]{1,0:T(4,128)}, f32[4,262144]{1,0:T(4,128)}, ...) fusion(f32[48,262144]{1,0:T(8,128)} %constant_dynamic-update-slice_fusion), kind=kLoop, calls=%fused_computation.850 | loop fusion | bytes 67108864 | tf_op jit(solution)/shard_map/slice | solution.py:57
  912.5 7.6 reshape.2090
  931.1 6.8 fusion.209
  971.2 7.9 rev.14
  981.9 5.9 copy.169
  999.0 43.1 %all-gather.13.cloned.1.call-done = f32[1024,512]{1,0:T(8,128)} async-done(((f32[128,512]{1,0:T(8,128)}), f32[1024,512]{1,0:T(8,128)}) %all-gather.13.cloned.1.call-update) | async-done | bytes 2097168 | tf_op jit(solution)/shard_map/all_gather | solution.py:283
  1050.3 22.8 while.174
  1094.4 7.1 reshape.2103
  1101.6 7.1 reshape.2101
  1114.2 5.7 copy.174
  1122.8 6.8 fusion.244
  1172.9 7.1 reshape.2112
  1192.4 5.8 rev.15
  1202.2 6.3 copy.184
  1216.8 26.5 all-gather.17.cloned.1.call-done
  1251.6 23.4 while.175
  1253.9 5.8 fusion.672
  1265.7 5.8 fusion.672
  1283.9 23.7 while.170
  1286.3 5.8 fusion.626
  1298.1 5.8 fusion.626
  1311.0 6.8 fusion.248
  1361.0 155.6 %while.171 = (s32[]{:T(128)}, f32[128,8,64]{0,2,1:T(8,128)}, f32[8,128,1280]{2,1,0:T(8,128)}, f32[8,128,1]{1,2,0:T(1,128)S(1)}, f32[8,128,1]{1,2,0:T(1,128)S(1)}...) while((s32[]{:T(128)}, f32[128,8,64]{0,2,1:T(8,128)}, ...), condition=%wide.region_58.59_spmd.clone.clone.clone, body=%wide.region_51.58_spmd.clone.clone.clone.sunk | while | flops 2032299392 | bytes 58498064 | solution.py:209
  1388.5 19.6 dynamic_update_slice.165
  1408.2 19.6 dynamic_update_slice.166
  1427.7 9.4 add_any.910
  1465.7 19.6 dynamic_update_slice.165
  1485.3 19.6 dynamic_update_slice.166
  1504.9 11.3 add_any.910
  1526.1 23.1 while.172
  1528.5 5.6 fusion.646
  1550.5 6.0 rev.16
  1567.3 23.4 reduce-scatter.7.cloned.1.call-done
  1593.2 68.9 %reduce-scatter.9.cloned.1.call-done = f32[128,512]{0,1:T(8,128)} async-done(((f32[1024,512]{0,1:T(8,128)}), f32[128,512]{0,1:T(8,128)}) %reduce-scatter.9.cloned.1.call-update) | async-done | bytes 262160 | tf_op jit(solution)/shard_map/reduce_scatter | solution.py:375
  1710.7 156.6 %while.173 = (s32[]{:T(128)}, f32[128,8,64]{0,2,1:T(8,128)}, f32[8,128,1280]{2,1,0:T(8,128)}, f32[8,128,1]{1,2,0:T(1,128)S(1)}, f32[8,128,1]{1,2,0:T(1,128)S(1)}...) while((s32[]{:T(128)}, f32[128,8,64]{0,2,1:T(8,128)}, ...), condition=%wide.region_85.86_spmd.clone.clone.clone, body=%wide.region_78.85_spmd.clone.clone.clone.sunk | while | flops 2032299392 | bytes 58498064 | solution.py:209
  1738.7 19.6 dynamic_update_slice.169
  1758.3 19.6 dynamic_update_slice.170
  1777.9 9.4 add_any.922
  1816.4 19.6 dynamic_update_slice.169
  1836.0 19.6 dynamic_update_slice.170
  1855.6 11.3 add_any.922
  1890.4 8.2 copy.456
  1950.8 8.1 copy.446
  1968.3 8.2 copy.447
  2003.5 8.8 reduce-scatter.13.cloned.1.call-done
  2017.9 5.7 fusion.150
  2046.4 8.4 copy.437
  2054.8 122.2 %concatenate.108 = f32[48,262144]{1,0:T(8,128)} concatenate(f32[8,262144]{1,0:T(8,128)} %bitcast.806, f32[1,262144]{1,0:T(1,128)} %bitcast.850, f32[1,262144]{1,0:T(1,128)} %bitcast.851, f32[1,262144]{1,0:T(1,128)} %bitcast.852, f32[1,262144]{1,0:T(1,128)} %bitcast.846, f32[1,262144]{1,0:T(1,128)} %bitcast.849, f32[1,262144]{1,0:T(1,128)} %bitcast.848, f32[1,262144]{1,0:T(1,128)} %bitcast.847, ...), dimensions={0} | concatenate | bytes 100663296 | tf_op jit(solution)/shard_map/concatenate | solution.py:433
  2185.0 781.3 %reduce-scatter.15.cloned.1.call-done = f32[48,32768]{1,0:T(8,128)} async-done(((f32[48,262144]{1,0:T(8,128)}), f32[48,32768]{1,0:T(8,128)}) %reduce-scatter.15.cloned.1.call-update) | async-done | bytes 6291472 | tf_op jit(solution)/shard_map/reduce_scatter | solution.py:435
  2966.3 10.1 scatter_custom_fusion
  2978.2 114.8 %all-reduce.58.cloned.1.call-done = f32[2,23,512]{2,1,0:T(8,128)} async-done(((f32[2,23,512]{2,1,0:T(8,128)}), f32[2,23,512]{2,1,0:T(8,128)}) %all-reduce.58.cloned.1.call-update) | async-done | bytes 94224 | tf_op jit(solution)/shard_map/psum | solution.py:438
  3096.9 71.4 %reduce-scatter.17.cloned.1.call-done = f32[16,32768]{1,0:T(8,128)} async-done(((f32[64,32768]{1,0:T(8,128)}), f32[16,32768]{1,0:T(8,128)}) %reduce-scatter.17.cloned.1.call-update) | async-done | bytes 2097168 | tf_op jit(solution)/shard_map/reduce_scatter | solution.py:437
  3168.3 7.3 multiply_add_fusion.4
  (1462 shorter events, 629.3 us)
Async XLA Ops:
  7.2 233.3 %all-gather.7.cloned.1.call-start = ((), (), s32[]{:S(2)}) async-start(), calls=%async_computation.6 | async-start | bytes 18874368 | tf_op jit(solution)/shard_map/all_gather | solution.py:260
  7.9 625.1 %all-gather.9.cloned.1.call-start = ((), (), s32[]{:S(2)}) async-start(), calls=%async_computation.7 | async-start | bytes 83886080 | tf_op jit(solution)/shard_map/all_gather | solution.py:261
  240.6 751.2 %all-gather.11.cloned.1.call-start = ((), (), s32[]{:S(2)}) async-start(), calls=%async_computation.8 | async-start | bytes 2359296 | tf_op jit(solution)/shard_map/all_gather | solution.py:282
  940.5 132.8 %copy-start.13 = (f32[128,512]{1,0:T(8,128)}, f32[128,512]{1,0:T(8,128)S(1)}, u32[]{:S(2)}) copy-start(f32[128,512]{1,0:T(8,128)S(1)} %get-tuple-element.4660) | copy-start | bytes 786436
  942.3 99.8 %all-gather.13.cloned.1.call-start = ((), (), s32[]{:S(2)}) async-start(), calls=%async_computation.9 | async-start | bytes 2359296 | tf_op jit(solution)/shard_map/all_gather | solution.py:283
  945.7 262.8 %all-gather.15.cloned.1.call-start = ((), (), s32[]{:S(2)}) async-start(), calls=%async_computation.10 | async-start | bytes 2359296 | tf_op jit(solution)/shard_map/all_gather | solution.py:282
  947.0 232.9 %copy-start.179 = (f32[512]{0:T(512)}, f32[512]{0:T(512)S(1)}, u32[]{:S(2)}) copy-start(f32[512]{0:T(512)S(1)} %fusion.348) | copy-start | bytes 6148
  948.5 234.7 %copy-start.169 = (f32[1,1,512]{2,0,1:T(1,128)}, f32[1,1,512]{2,0,1:T(1,128)S(1)}, u32[]{:S(2)}) copy-start(f32[1,1,512]{2,0,1:T(1,128)S(1)} %get-tuple-element.4620) | copy-start | bytes 6148
  948.5 329.9 %copy-start.185 = (f32[1,1,512]{2,0,1:T(1,128)}, f32[1,1,512]{2,0,1:T(1,128)S(1)}, u32[]{:S(2)}) copy-start(f32[1,1,512]{2,0,1:T(1,128)S(1)} %get-tuple-element.4616) | copy-start | bytes 6148
  948.5 404.3 %copy-start.173 = (f32[1,1,512]{2,0,1:T(1,128)}, f32[1,1,512]{2,0,1:T(1,128)S(1)}, u32[]{:S(2)}) copy-start(f32[1,1,512]{2,0,1:T(1,128)S(1)} %get-tuple-element.4617) | copy-start | bytes 6148
  949.1 170.8 %copy-start.217 = (f32[1,1,512]{2,0,1:T(1,128)}, f32[1,1,512]{2,0,1:T(1,128)S(1)}, u32[]{:S(2)}) copy-start(f32[1,1,512]{2,0,1:T(1,128)S(1)} %get-tuple-element.4636) | copy-start | bytes 6148
  949.1 170.8 %copy-start.219 = (f32[1,1,512]{2,0,1:T(1,128)}, f32[1,1,512]{2,0,1:T(1,128)S(1)}, u32[]{:S(2)}) copy-start(f32[1,1,512]{2,0,1:T(1,128)S(1)} %get-tuple-element.4637) | copy-start | bytes 6148
  949.1 170.8 %copy-start.221 = (f32[1,1,512]{2,0,1:T(1,128)}, f32[1,1,512]{2,0,1:T(1,128)S(1)}, u32[]{:S(2)}) copy-start(f32[1,1,512]{2,0,1:T(1,128)S(1)} %get-tuple-element.4638) | copy-start | bytes 6148
  949.1 170.8 %copy-start.223 = (f32[1,1,512]{2,0,1:T(1,128)}, f32[1,1,512]{2,0,1:T(1,128)S(1)}, u32[]{:S(2)}) copy-start(f32[1,1,512]{2,0,1:T(1,128)S(1)} %get-tuple-element.4639) | copy-start | bytes 6148
  949.1 170.9 %copy-start.225 = (f32[1,1,512]{2,0,1:T(1,128)}, f32[1,1,512]{2,0,1:T(1,128)S(1)}, u32[]{:S(2)}) copy-start(f32[1,1,512]{2,0,1:T(1,128)S(1)} %get-tuple-element.4632) | copy-start | bytes 6148
  949.1 170.9 %copy-start.227 = (f32[1,1,512]{2,0,1:T(1,128)}, f32[1,1,512]{2,0,1:T(1,128)S(1)}, u32[]{:S(2)}) copy-start(f32[1,1,512]{2,0,1:T(1,128)S(1)} %get-tuple-element.4633) | copy-start | bytes 6148
  949.1 170.9 %copy-start.229 = (f32[1,1,512]{2,0,1:T(1,128)}, f32[1,1,512]{2,0,1:T(1,128)S(1)}, u32[]{:S(2)}) copy-start(f32[1,1,512]{2,0,1:T(1,128)S(1)} %get-tuple-element.4634) | copy-start | bytes 6148
  949.2 170.9 %copy-start.231 = (f32[1,1,512]{2,0,1:T(1,128)}, f32[1,1,512]{2,0,1:T(1,128)S(1)}, u32[]{:S(2)}) copy-start(f32[1,1,512]{2,0,1:T(1,128)S(1)} %get-tuple-element.4631) | copy-start | bytes 6148
  949.2 172.4 %copy-start.203 = (f32[1,1,512]{2,0,1:T(1,128)}, f32[1,1,512]{2,0,1:T(1,128)S(1)}, u32[]{:S(2)}) copy-start(f32[1,1,512]{2,0,1:T(1,128)S(1)} %get-tuple-element.4630) | copy-start | bytes 6148
  949.2 173.6 %copy-start.181 = (f32[1,1,512]{2,0,1:T(1,128)}, f32[1,1,512]{2,0,1:T(1,128)S(1)}, u32[]{:S(2)}) copy-start(f32[1,1,512]{2,0,1:T(1,128)S(1)} %get-tuple-element.4628) | copy-start | bytes 6148
  949.2 173.6 %copy-start.215 = (f32[1,1,512]{2,0,1:T(1,128)}, f32[1,1,512]{2,0,1:T(1,128)S(1)}, u32[]{:S(2)}) copy-start(f32[1,1,512]{2,0,1:T(1,128)S(1)} %get-tuple-element.4627) | copy-start | bytes 6148
  949.2 184.4 %copy-start.177 = (f32[1,1,512]{2,0,1:T(1,128)}, f32[1,1,512]{2,0,1:T(1,128)S(1)}, u32[]{:S(2)}) copy-start(f32[1,1,512]{2,0,1:T(1,128)S(1)} %get-tuple-element.4624) | copy-start | bytes 6148
  949.2 184.4 %copy-start.211 = (f32[1,1,512]{2,0,1:T(1,128)}, f32[1,1,512]{2,0,1:T(1,128)S(1)}, u32[]{:S(2)}) copy-start(f32[1,1,512]{2,0,1:T(1,128)S(1)} %get-tuple-element.4623) | copy-start | bytes 6148
  949.2 188.9 %copy-start.155 = (f32[1,1,512]{2,0,1:T(1,128)}, f32[1,1,512]{2,0,1:T(1,128)S(1)}, u32[]{:S(2)}) copy-start(f32[1,1,512]{2,0,1:T(1,128)S(1)} %get-tuple-element.4626) | copy-start | bytes 6148
  949.2 188.9 %copy-start.165 = (f32[1,1,512]{2,0,1:T(1,128)}, f32[1,1,512]{2,0,1:T(1,128)S(1)}, u32[]{:S(2)}) copy-start(f32[1,1,512]{2,0,1:T(1,128)S(1)} %get-tuple-element.4625) | copy-start | bytes 6148
  949.2 233.9 %copy-start.159 = (f32[1,1,512]{2,0,1:T(1,128)}, f32[1,1,512]{2,0,1:T(1,128)S(1)}, u32[]{:S(2)}) copy-start(f32[1,1,512]{2,0,1:T(1,128)S(1)} %get-tuple-element.4622) | copy-start | bytes 6148
  1076.3 45.2 %copy-start.25 = (f32[128,512]{1,0:T(8,128)}, f32[128,512]{1,0:T(8,128)S(1)}, u32[]{:S(2)}) copy-start(f32[128,512]{1,0:T(8,128)S(1)} %get-tuple-element.4662) | copy-start | bytes 786436
  1078.9 41.1 %copy-start.95 = (f32[128,512]{1,0:T(8,128)}, f32[128,512]{1,0:T(8,128)S(1)}, u32[]{:S(2)}) copy-start(f32[128,512]{1,0:T(8,128)S(1)} %get-tuple-element.4663) | copy-start | bytes 786436
  1078.9 41.0 %collective-permute-start = (f32[4,512]{1,0:T(4,128)S(1)}, f32[4,512]{1,0:T(4,128)S(1)}, u32[]{:S(2)}, u32[]{:S(2)}) collective-permute-start(f32[4,512]{1,0:T(4,128)S(1)} %get-tuple-element.4598), channel_id=1, source_target_pairs={{0,4},{4,8},{8,12},{12,16},{16,20},{20,24},{24,28},{1,5},{5,9},{9,... | collective-permute-start | bytes 24584 | tf_op jit(solution)/shard_map/ppermute | solution.py:33
  1081.4 38.5 %collective-permute-start.1 = (f32[4,512]{1,0:T(4,128)S(1)}, f32[4,512]{1,0:T(4,128)S(1)}, u32[]{:S(2)}, u32[]{:S(2)}) collective-permute-start(f32[4,512]{1,0:T(4,128)S(1)} %get-tuple-element.4599), channel_id=1, source_target_pairs={{4,0},{8,4},{12,8},{16,12},{20,16},{24,20},{28,24},{5,1},{9,5},{13... | collective-permute-start | bytes 24584 | tf_op jit(solution)/shard_map/ppermute | solution.py:36
  1093.1 48.1 %copy-start.50 = (f32[512,512]{1,0:T(8,128)}, f32[512,512]{1,0:T(8,128)S(1)}, u32[]{:S(2)}) copy-start(f32[512,512]{1,0:T(8,128)S(1)} %squeeze.340) | copy-start | bytes 3145732
  1141.0 134.1 %copy-start.20 = (f32[128,512]{1,0:T(8,128)}, f32[128,512]{1,0:T(8,128)S(1)}, u32[]{:S(2)}) copy-start(f32[128,512]{1,0:T(8,128)S(1)} %get-tuple-element.4670) | copy-start | bytes 786436
  1141.0 42.2 %copy-start.189 = (f32[128]{0:T(128)}, f32[128]{0:T(128)S(1)}, u32[]{:S(2)}) copy-start(f32[128]{0:T(128)S(1)} %broadcast_multiply_fusion.6) | copy-start | bytes 1540
  1141.2 41.9 %copy-start.199 = (f32[128]{0:T(128)}, f32[128]{0:T(128)S(1)}, u32[]{:S(2)}) copy-start(f32[128]{0:T(128)S(1)} %fusion.363) | copy-start | bytes 1540
  1142.7 100.6 %all-gather.17.cloned.1.call-start = ((), (), s32[]{:S(2)}) async-start(), calls=%async_computation.11 | async-start | bytes 2359296 | tf_op jit(solution)/shard_map/all_gather | solution.py:283
  1144.5 446.2 %reduce-scatter.7.cloned.1.call-start = ((), (), s32[]{:S(2)}) async-start(), calls=%async_computation.12 | async-start | bytes 2359296 | tf_op jit(solution)/shard_map/reduce_scatter | solution.py:376
  1277.3 75.5 %copy-start.28 = (f32[128,512]{1,0:T(8,128)}, f32[128,512]{1,0:T(8,128)S(1)}, u32[]{:S(2)}) copy-start(f32[128,512]{1,0:T(8,128)S(1)} %get-tuple-element.4672) | copy-start | bytes 786436
  1277.3 75.5 %copy-start.209 = (f32[128]{0:T(128)}, f32[128]{0:T(128)S(1)}, u32[]{:S(2)}) copy-start(f32[128]{0:T(128)S(1)} %broadcast_multiply_fusion.5) | copy-start | bytes 1540
  1277.5 75.3 %copy-start.247 = (f32[128]{0:T(128)}, f32[128]{0:T(128)S(1)}, u32[]{:S(2)}) copy-start(f32[128]{0:T(128)S(1)} %fusion.364) | copy-start | bytes 1540
  1278.4 72.6 %copy-start.68 = (f32[128,512]{1,0:T(8,128)}, f32[128,512]{1,0:T(8,128)S(1)}, u32[]{:S(2)}) copy-start(f32[128,512]{1,0:T(8,128)S(1)} %fusion.134) | copy-start | bytes 786436
  1279.9 27.7 collective-permute-start.2
  1282.3 25.3 collective-permute-start.3
  1338.3 6.3 collective-permute-start.4
  1343.3 6.4 collective-permute-start.5
  1520.0 142.1 %reduce-scatter.9.cloned.1.call-start = ((), (), s32[]{:S(2)}) async-start(), calls=%async_computation.13 | async-start | bytes 2359296 | tf_op jit(solution)/shard_map/reduce_scatter | solution.py:375
  1524.4 476.9 %reduce-scatter.11.cloned.1.call-start = ((), (), s32[]{:S(2)}) async-start(), calls=%async_computation.14 | async-start | bytes 2359296 | tf_op jit(solution)/shard_map/reduce_scatter | solution.py:376
  1562.4 99.7 %copy-start.51 = (f32[512,512]{1,0:T(8,128)S(1)}, f32[512,512]{1,0:T(8,128)}, u32[]{:S(2)}) copy-start(f32[512,512]{1,0:T(8,128)} %copy-done.50) | copy-start | bytes 3145732
  1565.0 99.5 %copy-start.21 = (f32[128,512]{1,0:T(8,128)S(1)}, f32[128,512]{1,0:T(8,128)}, u32[]{:S(2)}) copy-start(f32[128,512]{1,0:T(8,128)} %copy-done.20) | copy-start | bytes 786436
  1565.0 99.5 %copy-start.160 = (f32[1,1,512]{2,0,1:T(1,128)S(1)}, f32[1,1,512]{2,0,1:T(1,128)}, u32[]{:S(2)}) copy-start(f32[1,1,512]{2,0,1:T(1,128)} %copy-done.159) | copy-start | bytes 6148
  1565.0 99.5 %copy-start.190 = (f32[128]{0:T(128)S(1)}, f32[128]{0:T(128)}, u32[]{:S(2)}) copy-start(f32[128]{0:T(128)} %copy-done.189) | copy-start | bytes 1540
  1565.0 99.5 %copy-start.200 = (f32[128]{0:T(128)S(1)}, f32[128]{0:T(128)}, u32[]{:S(2)}) copy-start(f32[128]{0:T(128)} %copy-done.199) | copy-start | bytes 1540
  1567.3 100.3 %copy-start.120 = (f32[128,8,64]{0,2,1:T(8,128)}, f32[128,8,64]{0,2,1:T(8,128)S(1)}, u32[]{:S(2)}) copy-start(f32[128,8,64]{0,2,1:T(8,128)S(1)} %get-tuple-element.4588) | copy-start | bytes 786436
  1593.2 74.3 %copy-start.384 = (f32[128]{0:T(128)S(1)}, f32[128]{0:T(128)}, u32[]{:S(2)}) copy-start(f32[128]{0:T(128)} %copy-done.383) | copy-start | bytes 1540
  1593.2 74.6 %copy-start.108 = (f32[128,512]{1,0:T(8,128)S(1)}, f32[128,512]{1,0:T(8,128)}, u32[]{:S(2)}) copy-start(f32[128,512]{1,0:T(8,128)} %copy-done.107) | copy-start | bytes 786436
  1691.2 4.1 collective-permute-start.6
  1694.0 5.5 collective-permute-start.7
  1870.8 141.5 %reduce-scatter.13.cloned.1.call-start = ((), (), s32[]{:S(2)}) async-start(), calls=%async_computation.15 | async-start | bytes 2359296 | tf_op jit(solution)/shard_map/reduce_scatter | solution.py:375
  1918.6 1047.7 %reduce-scatter.15.cloned.1.call-start = ((), (), s32[]{:S(2)}) async-start(), calls=%async_computation.16 | async-start | bytes 56623104 | tf_op jit(solution)/shard_map/reduce_scatter | solution.py:435
  2177.4 915.6 %all-reduce.58.cloned.1.call-start = ((), (), s32[]{:S(2)}) async-start(), calls=%async_computation.18 | async-start | bytes 196608 | tf_op jit(solution)/shard_map/psum | solution.py:438
  2184.9 983.3 %reduce-scatter.17.cloned.1.call-start = ((), (), s32[]{:S(2)}) async-start(), calls=%async_computation.17 | async-start | bytes 10485760 | tf_op jit(solution)/shard_map/reduce_scatter | solution.py:437
  2976.4 116.5 %copy-start.154 = (f32[2,23,512]{2,0,1:T(2,128)S(1)}, f32[2,23,512]{2,0,1:T(2,128)}, u32[]{:S(2)}) copy-start(f32[2,23,512]{2,0,1:T(2,128)} %param.42) | copy-start | bytes 282628
  2976.5 116.5 %copy-start.175 = (f32[2,23,512]{2,0,1:T(2,128)S(1)}, f32[2,23,512]{2,0,1:T(2,128)}, u32[]{:S(2)}) copy-start(f32[2,23,512]{2,0,1:T(2,128)} %param.45) | copy-start | bytes 282628
  2976.5 116.5 %copy-start.176 = (f32[2,23,512]{2,0,1:T(2,128)S(1)}, f32[2,23,512]{2,0,1:T(2,128)}, u32[]{:S(2)}) copy-start(f32[2,23,512]{2,0,1:T(2,128)} %param.43) | copy-start | bytes 282628
  2976.5 191.8 %copy-start.78 = (f32[16,32768]{1,0:T(8,128)S(1)}, f32[16,32768]{1,0:T(8,128)}, u32[]{:S(2)}) copy-start(f32[16,32768]{1,0:T(8,128)} %param.38) | copy-start | bytes 6291460
  (370 other events, 2382.0 us)
Sparse Core Ops, SparseCore 0:
  10.2 230.2 all-gather.6
  242.1 390.8 all-gather.8
  942.4 49.2 all-gather.10
  994.3 47.7 all-gather.12
  1142.9 50.5 all-gather.14
  1195.5 47.8 all-gather.16
  1520.1 70.4 reduce-scatter.6
  1594.7 67.3 reduce-scatter.8
  1870.9 69.9 reduce-scatter.10
  1944.8 67.3 reduce-scatter.12
  2177.5 788.7 reduce-scatter.14
  2973.2 119.6 all-reduce.57
  3095.7 72.5 reduce-scatter.16
where the time goes:
time: 3220 us; the launch traced here: 3180 us
  waiting for transfers between devices  1770 us (55%)
  local copies, waits for them, and re-layouts  956 us (30%)
  matrix products  324 us (10%)
  other arithmetic  81.1 us (3%)
    reduce_scatter x1, waiting for transfers between devices, on_device(): lax.psum_scatter(block_grads, 'seq', scatter_dimension=1, tiled=True)  781 us
    all_gather x1, waiting for transfers between devices, on_device(): slot_rows = lax.all_gather(columns, 'grp', axis=0, tiled=True)  388 us
    all_gather x1, waiting for transfers between devices, on_device(): columns = lax.all_gather(master, 'seq', axis=1, tiled=True)  233 us
    dot_general x70, matrix products, product(): return jnp.dot(left, right, precision=PRECISION_HIGH)  181 us
    unnamed x833, local copies, waits for them, and re-layouts  176 us
    dynamic_update_slice x16, local copies, waits for them, and re-layouts, attention_core(): lax.scan(jax.checkpoint(visit), initial, (key_blocks, value_blocks, item_...  169 us
    gather x5, local copies, waits for them, and re-layouts, on_device(): blocks_all = slot_rows[slot_of].reshape(-1, hidden_width, hidden_width)  122 us
    concatenate x1, local copies, waits for them, and re-layouts, on_device(): jnp.concatenate(layer_blocks, axis=0).reshape(blocks_all.shape[0], -1)  122 us
  transfers between devices with their start and end apart: 21, of which 13 were waited for; matrix products, arithmetic and copies ran while one was open for 12% of the time, Pallas kernels for 0%

commit v1 on v0

v1 whole, which is shorter than its diff:
```python
import functools
import math

import jax
import jax.numpy as jnp
import numpy as np
from jax import lax
from jax.experimental import pallas as pl
from jax.experimental.pallas import tpu as pltpu
from jax.sharding import PartitionSpec as P

HEADS = 8
KERNEL = 9
NB = 128
L = 2
CAP = 16
STEP = 10
EPS_NORM = 1e-05
BETA_ONE = 0.9
BETA_TWO = 0.999
ADAM_EPS = 1e-08
RATE_MATRIX = 0.03
RATE_SMALL = 0.1
DECAY_WEIGHT = 0.01
AVERAGE_KEEP = 0.99


def position_tables(width):
    falling = NB // 2 - 1 - np.arange(NB)
    doubled = np.clip(2 * falling, -(NB // 2), NB // 2 - 1)
    offset = np.concatenate([falling, doubled]).astype(np.float64)[:, None]
    column = np.arange(width)
    frequency = np.exp(-math.log(10000.0) * (2 * (column // 2)) / width)[None, :]
    angles = offset * frequency
    return jnp.asarray(np.where(column[None, :] % 2 == 0, np.sin(angles), np.cos(angles)), jnp.float32)


def frame_info(frame_index, lengths_row, flags_row):
    item_ends = jnp.cumsum(lengths_row)
    item_starts = item_ends - lengths_row
    inside = (frame_index[:, None] >= item_starts[None, :]) & (
        frame_index[:, None] < item_ends[None, :]
    )
    numbers = jnp.arange(lengths_row.shape[0], dtype=jnp.int32)
    frame_items = jnp.sum(jnp.where(inside, numbers[None, :] + 1, 0), axis=1) - 1
    first_frame = jnp.sum(jnp.where(inside, item_starts[None, :], 0), axis=1)
    stride = jnp.sum(jnp.where(inside, 1 + flags_row[None, :], 0), axis=1)
    return (frame_items, (frame_index - first_frame) * stride)


def slot_index(owner_list):
    owners = owner_list[:, 0]
    numbers = jnp.arange(owners.shape[0], dtype=jnp.int32)
    earlier = (owners[None, :] == owners[:, None]) & (numbers[None, :] < numbers[:, None])
    owner_rank = jnp.sum(earlier.astype(jnp.int32), axis=1)
    return owners * CAP + owner_rank


def adam_step(attention_weights, first_moment, second_moment, gradient, step_rate, decay_rate):
    first_moment = BETA_ONE * first_moment + (1.0 - BETA_ONE) * gradient
    second_moment = BETA_TWO * second_moment + (1.0 - BETA_TWO) * gradient * gradient
    fixed_one = 1.0 - BETA_ONE**STEP
    fixed_two = 1.0 - BETA_TWO**STEP
    direction = first_moment / fixed_one / (jnp.sqrt(second_moment / fixed_two) + ADAM_EPS)
    return (
        attention_weights - step_rate * (direction + decay_rate * attention_weights),
        first_moment,
        second_moment,
    )


MESH = pl.DeviceIdType.MESH
CHUNKS = 12
GROUP = 4


def places():
    seq = lax.axis_index("seq")
    grp = lax.axis_index("grp")
    return seq, grp, seq // 2, seq % 2, grp // 2, grp % 2


def over(lo, hi, fn):
    def body(i, carry):
        fn(i)
        return carry

    lax.fori_loop(lo, hi, body, 0)


def remote(src, dst, s, r, dev):
    return pltpu.make_async_remote_copy(
        src_ref=src, dst_ref=dst, send_sem=s, recv_sem=r, device_id=dev, device_id_type=MESH
    )


def update_kernel(
    block_ref, used_ref, shares_ref, master_ref, one_ref, two_ref, average_ref,
    new_master, copy, new_one, new_two, new_average, rows_ref, sems,
):
    i = pl.program_id(0)
    slots = master_ref.shape[0]

    def fetch(s):
        return pltpu.make_async_copy(shares_ref.at[block_ref[s]], rows_ref.at[s], sems.at[s])

    @pl.when(i == 0)
    def _():
        over(0, slots, lambda s: fetch(s).start())
        over(0, slots, lambda s: fetch(s).wait())

    half = rows_ref.shape[-1]
    pieces = []
    for r in range(8):
        for h in range(2):
            pieces.append(rows_ref[:, h, i * 8 + r, :])
    gradient = jnp.concatenate(pieces, axis=1) * used_ref[...]
    master = master_ref[...]
    master, one, two = adam_step(
        master, one_ref[...], two_ref[...], gradient, RATE_MATRIX, DECAY_WEIGHT
    )
    new_master[...] = master
    copy[...] = master.astype(jnp.bfloat16)
    new_one[...] = one
    new_two[...] = two
    new_average[...] = AVERAGE_KEEP * average_ref[...] + (1.0 - AVERAGE_KEEP) * master


def update_slots(shares, block, used, master, moment_one, moment_two, average):
    slab, half = shares.shape[2:]
    slots, entries = master.shape
    columns = 8 * 2 * half
    spec = pl.BlockSpec((slots, columns), lambda i, block: (0, i))
    full = jax.ShapeDtypeStruct((slots, entries), jnp.float32)
    return pl.pallas_call(
        update_kernel,
        grid_spec=pltpu.PrefetchScalarGridSpec(
            num_scalar_prefetch=1,
            grid=(slab // 8,),
            in_specs=[
                pl.BlockSpec((slots, 1), lambda i, block: (0, 0)), pl.BlockSpec(memory_space=pl.ANY),
                spec, spec, spec, spec,
            ],
            out_specs=[spec] * 5,
            scratch_shapes=[
                pltpu.VMEM((slots, 2, slab, half), jnp.float32), pltpu.SemaphoreType.DMA((slots,)),
            ],
        ),
        out_shape=[full, jax.ShapeDtypeStruct((slots, entries), jnp.bfloat16), full, full, full],
        compiler_params=pltpu.CompilerParams(vmem_limit_bytes=LIMIT),
        name="update_slots",
    )(block, used, shares, master, moment_one, moment_two, average)


BF16 = jnp.bfloat16
F32 = jnp.float32
ROWS = 32
KEYS = 1024


def split(value):
    high = value.astype(BF16)
    return high, (value - high.astype(F32)).astype(BF16)


def dot(left, right, dims):
    return lax.dot_general(left, right, (dims, ((), ())), preferred_element_type=F32)


def dot3(left, right, dims):
    (lh, ll), (rh, rl) = left, right
    rows = lh.shape[0]
    if dims[0] == (1,) and rows <= 128:
        both = dot(jnp.concatenate([lh, ll], axis=0), rh, dims)
        return both[:rows] + (both[rows:] + dot(lh, rl, dims))
    return dot(lh, rh, dims) + (dot(ll, rh, dims) + dot(lh, rl, dims))


def nn(left, right):
    return dot3(left, right, ((1,), (0,)))


def nt(left, right):
    return dot3(left, right, ((1,), (1,)))


def tn(left, right):
    (lh, ll), (rh, rl) = left, right
    return dot(
        jnp.concatenate([lh, lh, ll], axis=0),
        jnp.concatenate([rh, rl, rh], axis=0),
        ((0,), (0,)),
    )


def tn_long(left, right):
    return dot3(left, right, ((0,), (0,)))


def norm(value):
    center = value - jnp.mean(value, axis=-1, keepdims=True)
    scale = lax.rsqrt(jnp.mean(center * center, axis=-1, keepdims=True) + EPS_NORM)
    return center * scale, scale


def norm_back(grad, unit, scale, gain):
    inner = grad * gain
    value_grad = scale * (
        inner
        - jnp.mean(inner, axis=-1, keepdims=True)
        - unit * jnp.mean(inner * unit, axis=-1, keepdims=True)
    )
    return (
        value_grad,
        jnp.sum(grad * unit, axis=0, keepdims=True),
        jnp.sum(grad, axis=0, keepdims=True),
    )


def sigmoid(value):
    return 1.0 / (1.0 + jnp.exp(-value))


def ffn_forward(v, small, row, weights, first, z_ref, middle=None):
    unit, _ = norm(v)
    h = split(unit * small[row : row + 1] + small[row + 1 : row + 2])
    total = None
    for j in range(4):
        z = nn(h, split(weights.get(first + j)))
        z_ref[:, 512 * j : 512 * j + 512] = z
        part = nn(split(z * sigmoid(z)), split(weights.get(first + 4 + j)))
        total = part if total is None else total + part
        if j == 1 and middle is not None:
            middle()
    return v + 0.5 * total


def ffn_backward(grad, v, z_ref, small, row, weights, first, grads, at, ds_ref, middle):
    unit, scale = norm(v)
    gain = small[row : row + 1]
    hth, htl = split((unit * gain + small[row + 1 : row + 2]).T)
    wide = jnp.concatenate([hth, hth, htl], axis=1)
    half = split(0.5 * grad)
    for j in range(4):
        z = z_ref[:, 512 * j : 512 * j + 512]
        grads.put(at + 4 + j, tn(split(z * sigmoid(z)), half))
    middle()
    total = None
    for j in range(4):
        z = z_ref[:, 512 * j : 512 * j + 512]
        s = sigmoid(z)
        da = nt(half, split(weights.get(first + 4 + j)))
        dz = split(da * (s * (1.0 + z * (1.0 - s))))
        tall = jnp.concatenate([dz[0], dz[1], dz[0]], axis=0)
        grads.put(at + j, dot(wide, tall, ((1,), (0,))))
        part = nt(dz, split(weights.get(first + j)))
        total = part if total is None else total + part
    back, dg, dc = norm_back(total, unit, scale, gain)
    ds_ref[row : row + 1] = dg
    ds_ref[row + 1 : row + 2] = dc
    return grad + back


def conv_mix(ext_ref, masks, small):
    mixed = None
    for t in range(KERNEL):
        part = ext_ref[t : t + masks.shape[0], :] * masks[:, t : t + 1] * small[12 + t : 13 + t]
        mixed = part if mixed is None else mixed + part
    return mixed


def conv_forward(v, ext_ref, masks, small, wc):
    unit, _ = norm(conv_mix(ext_ref, masks, small))
    n = unit * small[6:7] + small[7:8]
    return v + nn(split(n * sigmoid(n)), split(wc))


def conv_backward(grad, ext_ref, masks, small, wc, grads, at, dext_ref, ds_ref):
    unit, scale = norm(conv_mix(ext_ref, masks, small))
    gain = small[6:7]
    n = unit * gain + small[7:8]
    s = sigmoid(n)
    g = split(grad)
    grads.put(at, tn(split(n * s), g))
    dn = nt(g, split(wc)) * (s * (1.0 + n * (1.0 - s)))
    dm, dg, dc = norm_back(dn, unit, scale, gain)
    ds_ref[6:7] = dg
    ds_ref[7:8] = dc
    rows = masks.shape[0]
    dext_ref[...] = jnp.zeros_like(dext_ref)
    for t in range(KERNEL):
        dmt = dm * masks[:, t : t + 1]
        ds_ref[12 + t : 13 + t] = jnp.sum(dmt * ext_ref[t : t + rows, :], axis=0, keepdims=True)
        dext_ref[t : t + rows, :] += dmt * small[12 + t : 13 + t]


def fill_ext(ext_ref, low, middle, high):
    half = (KERNEL - 1) // 2
    rows = middle.shape[0]
    ext_ref[0:half, :] = low
    ext_ref[half : half + rows, :] = middle
    ext_ref[half + rows : 2 * half + rows, :] = high


def gate_forward(v, small, wa, wg):
    unit, _ = norm(v)
    h = split(unit * small[4:5] + small[5:6])
    za, zg = nn(h, split(wa)), nn(h, split(wg))
    return za, zg, za * sigmoid(zg)


def gate_backward(grad_glu, grad, v, za, zg, small, wa, wg, grads, at, ds_ref):
    unit, scale = norm(v)
    gain = small[4:5]
    h = split(unit * gain + small[5:6])
    s = sigmoid(zg)
    da = split(grad_glu * s)
    dg_ = split(grad_glu * za * s * (1.0 - s))
    grads.put(at, tn(h, da))
    grads.put(at + 1, tn(h, dg_))
    back, dg, dc = norm_back(nt(da, split(wa)) + nt(dg_, split(wg)), unit, scale, gain)
    ds_ref[4:5] = dg
    ds_ref[5:6] = dc
    return grad + back


def stacked(quad):
    rows = quad.shape[0]
    tall = jnp.concatenate([quad] * 4, axis=0)
    shape = (4 * rows, 256)
    head = lax.broadcasted_iota(jnp.int32, shape, 0) // rows
    lane = lax.broadcasted_iota(jnp.int32, shape, 1) // 64
    return jnp.where(head == lane, tall, 0.0)


def unstacked(tall, rows):
    shape = (rows, 256)
    lane = lax.broadcasted_iota(jnp.int32, shape, 1) // 64
    quad = tall[0:rows]
    for n in range(1, 4):
        quad = jnp.where(lane == n, tall[n * rows : (n + 1) * rows], quad)
    return quad


def turned(value):
    rows = value.shape[0]
    shape = (rows, rows)
    place = lax.broadcasted_iota(jnp.int32, shape, 0) + lax.broadcasted_iota(jnp.int32, shape, 1)
    swap = jnp.where(place == rows - 1, 1.0, 0.0).astype(BF16)
    high, low = split(value)
    return dot(swap, high, ((1,), (0,))) + dot(swap, low, ((1,), (0,)))


def place_bias(quad_q, table, rate, bias_ref, head0):
    rows = quad_q.shape[0]
    near = nt(split(stacked(quad_q)), split(table))
    row = lax.broadcasted_iota(jnp.int32, (rows, 3 * rows), 0)
    column = lax.broadcasted_iota(jnp.int32, (rows, 3 * rows), 1)
    place = column - row - 65
    for n in range(4):
        both = near[n * rows : (n + 1) * rows]
        one = jnp.where(rate == 2, both[:, 128:], both[:, :128])
        last, first = one[:, 0:1], one[:, 127:128]
        wide = jnp.concatenate([one, jnp.zeros((rows, 2 * rows), F32)], axis=1)
        rolled = pltpu.roll(wide, 65, 1, stride=1, stride_axis=0)
        window = jnp.where(place < 0, last, jnp.where(place > 127, first, rolled))
        bias_ref[head0 + n, 0] = jnp.broadcast_to(last, (rows, rows))
        for i in range(3):
            bias_ref[head0 + n, 1 + i] = window[:, i * rows : (i + 1) * rows]
        bias_ref[head0 + n, 4] = jnp.broadcast_to(first, (rows, rows))


def tile_scores(s_ref, bias_ref, items_q, items_k, tile, head0, own, chunk, rows):
    per = rows // ROWS
    head, part = tile // per, tile % per
    r0 = pl.multiple_of(part * ROWS, ROWS)
    s0 = pl.multiple_of(tile * ROWS, ROWS)
    iq = items_q[pl.ds(r0, ROWS), :]
    tiles = []
    keys = s_ref.shape[1]
    for jt in range(keys // rows):
        kind = jnp.clip(chunk * (keys // rows) + jt - own + 2, 0, 4)
        bias = bias_ref[head0 + head, kind, pl.ds(r0, ROWS), :]
        tiles.append(s_ref[pl.ds(s0, ROWS), jt * rows : (jt + 1) * rows] + bias)
    scores = jnp.concatenate(tiles, axis=1) * 0.125
    return scores, iq == items_k, s0, r0


def vmem(*shape, dtype=jnp.float32):
    return pltpu.VMEM(shape, dtype)


def shape_of(*shape):
    return jax.ShapeDtypeStruct(shape, jnp.float32)


WHOLE = pl.BlockSpec(memory_space=pltpu.VMEM)
FAR = pl.BlockSpec(memory_space=pl.ANY)
LIMIT = 62 * 1024 * 1024


ORDER = (0, 1, 2, 3, 4, 5, 6, 7, 8, 12, 9, 10, 11, 13, 14, 15, 16, 17, 18, 19, 20, 21, 22, 23)
PQ, PP, PK, PV, PO, PA, PG, PC = range(8, 16)
PER = 6
RIM = 8
X, V1, V2, CTX, Q, ZA, ZG, GLU, V3, V4 = range(10)


def signal_rims(barrier, seq, count):
    for to in ((seq + 1) % count, (seq + count - 1) % count):
        pl.semaphore_signal(barrier, inc=1, device_id={"seq": to}, device_id_type=MESH)


def enter_all(seq, grp, zs):
    y, z = seq % 2, seq // 2
    barrier = pltpu.get_barrier_semaphore()
    for peer in (grp + 1 - 2 * (grp % 2), (grp + 2) % 4):
        pl.semaphore_signal(barrier, inc=1, device_id={"grp": peer}, device_id_type=MESH)
    pl.semaphore_signal(barrier, inc=1, device_id={"seq": z * 2 + 1 - y}, device_id_type=MESH)

    def greet(d):
        pl.semaphore_signal(
            barrier, inc=1, device_id={"seq": ((z + d) % zs) * 2 + y}, device_id_type=MESH
        )

    over(1, zs, greet)
    signal_rims(barrier, seq, 2 * zs)
    pl.semaphore_wait(barrier, zs + 4)


def joined(halves):
    size = halves.shape[1] * halves.shape[2] * halves.shape[3]
    return jnp.concatenate([halves[i].reshape(size, halves.shape[-1]) for i in range(2)], axis=1)


class Gather:
    def __init__(self, zs, rows_ref, slot_ref, owned_ref, whole, table, sib, face, own, sems):
        self.zs = zs
        self.seq, self.grp, self.z, self.y, self.x, self.c = places()
        self.rows_ref, self.slot_ref, self.owned_ref = rows_ref, slot_ref, owned_ref
        self.whole, self.table, self.sib, self.face, self.own = whole, table, sib, face, own
        (
            self.local, self.sib_s, self.sib_r, self.face_s, self.face_r, self.z_s, self.z_r,
            self.a_s, self.a_r, self.b_s, self.b_r, self.c_s, self.c_r,
        ) = sems
        self.to_core = {"grp": self.grp + 1 - 2 * self.c}
        self.to_x = {"grp": (self.grp + 2) % 4}
        self.to_y = {"seq": self.z * 2 + 1 - self.y}
        self.place = 2 * self.c + self.x
        self.other = 2 * self.c + 1 - self.x

    def mine(self, place):
        return self.rows_ref[self.slot_ref[place]] * self.owned_ref[place]

    def sib_copy(self, k):
        return remote(self.table.at[k], self.sib.at[k], self.sib_s.at[k], self.sib_r.at[k], self.to_core)

    def face_copy(self, k):
        return remote(
            self.sib.at[k, 1 - self.x], self.face.at[k], self.face_s.at[k], self.face_r.at[k], self.to_x
        )

    def z_any(self, k, d, z):
        return remote(
            self.own.at[k], self.whole.at[GROUP * k + self.place, :, z, self.y], self.z_s.at[k, d], self.z_r.at[k, d],
            {"seq": ((self.z + d) % self.zs) * 2 + self.y},
        )

    def z_copy(self, k, d):
        return self.z_any(k, d, self.z)

    def z_arrival(self, k, d):
        return self.z_any(k, d, (self.z + self.zs - d) % self.zs)

    def keep(self, k):
        return pltpu.make_async_copy(
            self.own.at[k], self.whole.at[GROUP * k + self.place, :, self.z, self.y], self.local.at[k]
        )

    def two(self, k, parts, s, r):
        return [
            remote(part, part, s.at[k, i], r.at[k, i], to) for i, (part, to) in enumerate(parts)
        ]

    def a_any(self, k, first, second):
        parts = [(first, self.to_y), (second, self.to_x)]
        return self.two(k, parts, self.a_s, self.a_r)

    def a_copies(self, k):
        block = self.whole.at[GROUP * k + self.place]
        return self.a_any(k, block.at[0, :, self.y], block.at[1, :, self.y])

    def a_arrivals(self, k):
        return self.a_any(
            k,
            self.whole.at[GROUP * k + self.place, 0, :, 1 - self.y],
            self.whole.at[GROUP * k + self.other, 1, :, self.y],
        )

    def both(self, k, core):
        return pl.ds(GROUP * k + 2 * core, 2)

    def b_any(self, k, place, y):
        parts = [
            (self.whole.at[GROUP * k + place, 0], self.to_x),
            (self.whole.at[self.both(k, self.c), 1, :, y], self.to_y),
        ]
        return self.two(k, parts, self.b_s, self.b_r)

    def b_copies(self, k):
        return self.b_any(k, self.place, self.y)

    def b_arrivals(self, k):
        return self.b_any(k, self.other, 1 - self.y)

    def c_any(self, k, core):
        part = self.whole.at[self.both(k, core)]
        return remote(part, part, self.c_s.at[k], self.c_r.at[k], self.to_core)

    def begin(self, k):
        for i in range(2):
            self.table[k, i] = self.mine(GROUP * k + 2 * (1 - self.c) + i)
        self.sib_copy(k).start()

    def to_face(self, k):
        self.sib_copy(k).wait_recv()
        for i in range(2):
            self.sib[k, i] += self.mine(GROUP * k + 2 * self.c + i)
        self.face_copy(k).start()

    def to_z(self, k):
        self.face_copy(k).wait_recv()
        self.own[k] = self.sib[k, self.x] + self.face[k]
        over(1, self.zs, lambda d: self.z_copy(k, d).start())
        self.keep(k).start()

    def to_a(self, k):
        over(1, self.zs, lambda d: self.z_arrival(k, d).wait_recv())
        self.keep(k).wait()
        for copy in self.a_copies(k):
            copy.start()

    def to_b(self, k):
        for copy in self.a_arrivals(k):
            copy.wait_recv()
        for copy in self.b_copies(k):
            copy.start()

    def to_c(self, k):
        for copy in self.b_arrivals(k):
            copy.wait_recv()
        self.c_any(k, self.c).start()

    def open(self):
        over(0, CHUNKS, self.begin)
        over(0, 5, self.to_face)
        over(0, 3, self.to_z)

    def step(self, t):
        def stage(k, fn):
            @pl.when((k >= 0) & (k < CHUNKS))
            def _():
                fn(k)

        stage(t - 2, self.to_b)
        stage(t, self.to_a)
        stage(t - 3, self.to_c)
        stage(t + 5, self.to_face)
        stage(t + 3, self.to_z)

    def arrived(self, k):
        self.c_any(k, 1 - self.c).wait_recv()

    def finish(self, k):
        self.c_any(k, self.c).wait_send()
        for copy in self.a_copies(k) + self.b_copies(k):
            copy.wait_send()
        over(1, self.zs, lambda d: self.z_copy(k, d).wait_send())
        self.face_copy(k).wait_send()
        self.sib_copy(k).wait_send()


class Share:
    def __init__(self, zs, layer, source, out, keep_sem, z_s, z_r, y_s, y_r):
        self.zs, self.layer, self.source, self.out = zs, layer, source, out
        self.seq = lax.axis_index("seq")
        self.z, self.y = self.seq // 2, self.seq % 2
        self.sems = (keep_sem, z_s, z_r, y_s, y_r)

    def z_any(self, d, z, i):
        _, z_s, z_r, _, _ = self.sems
        block = self.out.at[self.layer, z * 2 + (self.y if i == 0 else 1 - self.y)]
        return remote(
            self.source if i == 0 else block, block, z_s.at[self.layer, d, i], z_r.at[self.layer, d, i],
            {"seq": ((self.z + d) % self.zs) * 2 + self.y},
        )

    def z_copy(self, d, i):
        return self.z_any(d, self.z, i)

    def z_arrival(self, d, i):
        return self.z_any(d, (self.z + self.zs - d) % self.zs, i)

    def y_any(self, y):
        _, _, _, y_s, y_r = self.sems
        return remote(
            self.source, self.out.at[self.layer, self.z * 2 + y], y_s.at[self.layer], y_r.at[self.layer],
            {"seq": self.z * 2 + 1 - self.y},
        )

    def keep(self):
        return pltpu.make_async_copy(
            self.source, self.out.at[self.layer, self.seq], self.sems[0].at[self.layer]
        )

    def start(self):
        self.y_any(self.y).start()
        over(1, self.zs, lambda d: self.z_copy(d, 0).start())
        self.keep().start()

    def forward(self):
        self.y_any(1 - self.y).wait_recv()
        over(1, self.zs, lambda d: self.z_copy(d, 1).start())

    def wait(self):
        for i in range(2):
            over(1, self.zs, lambda d: self.z_arrival(d, i).wait_recv())
        self.keep().wait()

    def finish(self):
        self.y_any(self.y).wait_send()
        for i in range(2):
            over(1, self.zs, lambda d: self.z_copy(d, i).wait_send())


class Rims:
    def __init__(self, count, layer, low, high, before, after, sems, recv):
        seq = lax.axis_index("seq")
        self.up = remote(
            high, before.at[layer], sems.at[layer, 0], recv.at[layer, 0], {"seq": (seq + 1) % count}
        )
        self.down = remote(
            low, after.at[layer], sems.at[layer, 1], recv.at[layer, 1], {"seq": (seq + count - 1) % count}
        )

    def start(self):
        self.up.start()
        self.down.start()

    def wait(self):
        self.up.wait_recv()
        self.down.wait_recv()

    def finish(self):
        self.up.wait_send()
        self.down.wait_send()


def forward_kernel(
    zs, chunks,
    rows_ref, slot_ref, owned_ref, x_ref, small_all, table_ref, iq_ref, ik_ref, rate_ref, masks_ref,
    whole, out_ref, rows_s, z_s, hs_s, k_s, val_s, lse_s, p_s, before_s, after_s, scores_s,
    table_w, sib, face, own_w, weights, x_v, kept, z_v, h_v, hs_v, k_v, val_v, p_v, lse_v, before, after, ext, bias_ref, s_ref, e_ref, top_ref, sum_ref, acc_ref,
    local, sib_sm, sib_rm, face_sm, face_rm, z_sm, z_rm, a_sm, a_rm, b_sm, b_rm, c_sm, c_rm,
    load_sems, save_sems, keep_sem, sz_s, sz_r, sy_s, sy_r, rim_s, rim_r, key_sems,
):
    seq = lax.axis_index("seq")
    grp = lax.axis_index("grp")
    count = 2 * zs
    enter_all(seq, grp, zs)
    gather = Gather(
        zs, rows_ref, slot_ref, owned_ref, whole, table_w, sib, face, own_w,
        (local, sib_sm, sib_rm, face_sm, face_rm, z_sm, z_rm, a_sm, a_rm, b_sm, b_rm, c_sm, c_rm),
    )
    gather.open()
    for t in range(5):
        gather.step(t)
    rows, width = x_ref.shape
    x_v[...] = x_ref[...]
    half = (KERNEL - 1) // 2
    slots = (0, 1, 2, 3, 0, 1)

    def layer_body(layer, carry):
        small = small_all.at[layer]

        def block(n):
            return joined(weights[slots[n // 4], n % 4])

        def load(i):
            return pltpu.make_async_copy(
                whole.at[pl.ds(GROUP * (PER * layer + i), GROUP)], weights.at[slots[i]], load_sems.at[slots[i]]
            )

        def saves(layer):
            pairs = [(kept, rows_s), (z_v, z_s), (lse_v, lse_s), (p_v, p_s)]
            return [
                pltpu.make_async_copy(v, s.at[layer], save_sems.at[i]) for i, (v, s) in enumerate(pairs)
            ]

        share = Share(zs, layer, h_v.at[layer], hs_s, keep_sem, sz_s, sz_r, sy_s, sy_r)
        rims = Rims(
            count, layer, kept.at[GLU, 0:RIM], kept.at[GLU, rows - RIM : rows], before, after, rim_s, rim_r
        )

        def steps(*numbers):
            for i in numbers:
                gather.step(PER * layer + i)

        def arrived(*numbers):
            for i in numbers:
                gather.arrived(PER * layer + i)
                load(i).start()

        class Held:
            def __init__(self):
                self.waited = set()

            def get(self, n):
                if n // 4 not in self.waited:
                    load(n // 4).wait()
                    self.waited.add(n // 4)
                return block(n)

        held = Held()
        arrived(0, 1)

        @pl.when(layer > 0)
        def _():
            for copy in saves(layer - 1):
                copy.wait()

        v1 = ffn_forward(x_v[...], small, 0, held, 0, z_v.at[0])
        kept[X] = x_v[...]
        kept[V1] = v1
        unit, _ = norm(v1)
        h_v[layer] = unit * small[2:3] + small[3:4]
        share.start()
        steps(5)
        arrived(2)
        q = nn(split(h_v[layer]), split(held.get(PQ)))
        kept[Q] = q
        table = nn(split(table_ref[...]), split(held.get(PP)))
        p_v[...] = table
        qv = q + small[22:23]
        for d in range(2):
            cols = slice(256 * d, 256 * d + 256)
            place_bias(qv[:, cols], table[:, cols], rate_ref[...], bias_ref, 4 * d)
        share.forward()
        steps(6, 7, 8)
        arrived(3)
        share.wait()
        attention_forward(
            chunks, count, layer, held, small, hs_s, k_s, val_s, scores_s, e_ref, hs_v, k_v, val_v, kept.at[Q], ik_ref, iq_ref,
            bias_ref, s_ref, top_ref, sum_ref, acc_ref, key_sems, rows, seq, lambda d: steps(9) if d == 0 else None,
        )
        lse_v[...] = top_ref[...] + jnp.log(sum_ref[...])
        for d in range(2):
            span = slice(4 * rows * d, 4 * rows * (d + 1))
            kept[CTX, :, 256 * d : 256 * d + 256] = unstacked(acc_ref[span, :] / sum_ref[span, :], rows)
        v2 = kept[V1] + nn(split(kept[CTX]), split(held.get(PO)))
        kept[V2] = v2
        za, zg, glu = gate_forward(v2, small, held.get(PA), held.get(PG))
        kept[ZA] = za
        kept[ZG] = zg
        kept[GLU] = glu
        rims.start()
        steps(10)
        arrived(4, 5)
        rims.wait()
        fill_ext(ext, before[layer, RIM - half : RIM, :], kept[GLU], after[layer, 0:half, :])
        v3 = conv_forward(kept[V2], ext, masks_ref[...], small, held.get(PC))
        kept[V3] = v3
        v4 = ffn_forward(v3, small, 8, held, 16, z_v.at[1])
        kept[V4] = v4
        unit, _ = norm(v4)
        x_v[...] = unit * small[10:11] + small[11:12]
        for copy in saves(layer):
            copy.start()
        rims.finish()
        share.finish()
        return carry

    lax.fori_loop(0, L, layer_body, 0)
    out_ref[...] = x_v[...]
    last = [
        pltpu.make_async_copy(v, s.at[L - 1], save_sems.at[i])
        for i, (v, s) in enumerate([(kept, rows_s), (z_v, z_s), (lse_v, lse_s), (p_v, p_s)])
    ]
    edges = [
        pltpu.make_async_copy(before, before_s, save_sems.at[4]),
        pltpu.make_async_copy(after, after_s, save_sems.at[5]),
    ]
    for copy in edges:
        copy.start()
    for copy in last + edges:
        copy.wait()

    over(0, CHUNKS, gather.finish)


def attention_forward(
    chunks, count, layer, held, small, hs_s, k_s, val_s, scores_s, e_ref, hs_v, k_v, val_v, q_v, ik_ref, iq_ref,
    bias_ref, s_ref, top_ref, sum_ref, acc_ref, key_sems, rows, own, between,
):
    per = KEYS // rows
    wk, wv = split(held.get(PK)), split(held.get(PV))
    if chunks > 1:
        top_ref[...] = jnp.full_like(top_ref, -1e30)
        sum_ref[...] = jnp.zeros_like(sum_ref)
        acc_ref[...] = jnp.zeros_like(acc_ref)

    def one(chunk):
        def fetch(b):
            return pltpu.make_async_copy(
                hs_s.at[layer, chunk * per + b],
                hs_v.at[pl.ds(pl.multiple_of(b * rows, rows), rows)],
                key_sems.at[b],
            )

        over(0, per, lambda b: fetch(b).start())
        over(0, per, lambda b: fetch(b).wait())
        hs = split(hs_v[...])
        k_v[...] = nn(hs, wk)
        val_v[...] = nn(hs, wv)
        span = pl.ds(pl.multiple_of(chunk * KEYS, KEYS), KEYS)
        out = [
            pltpu.make_async_copy(k_v, k_s.at[layer, span], key_sems.at[per]),
            pltpu.make_async_copy(val_v, val_s.at[layer, span], key_sems.at[per + 1]),
        ]
        for copy in out:
            copy.start()
        items_k = ik_ref[:, span] if chunks > 1 else ik_ref[...]
        for d in range(2):
            cols = slice(256 * d, 256 * d + 256)
            qs = split(stacked(q_v[:, cols] + small[21:22, cols]))
            s_ref[...] = nt(qs, split(k_v[:, cols]))

            def tile(i):
                scores, same, s0, _ = tile_scores(
                    s_ref, bias_ref, iq_ref, items_k, i, 4 * d, own, chunk, rows
                )
                scores = jnp.where(same, scores, -1e30)
                at_rows = pl.ds(pl.multiple_of(4 * rows * d + s0, ROWS), ROWS)
                top = jnp.max(scores, axis=-1, keepdims=True)
                if chunks > 1:
                    old = top_ref[at_rows, :]
                    top = jnp.maximum(top, old)
                    factor = jnp.exp(old - top)
                s_ref[pl.ds(s0, ROWS), :] = scores
                e = jnp.where(same, jnp.exp(scores - top), 0.0)
                total = jnp.sum(e, axis=-1, keepdims=True)
                if chunks > 1:
                    total = total + sum_ref[at_rows, :] * factor
                    acc_ref[at_rows, :] = acc_ref[at_rows, :] * factor
                top_ref[at_rows, :] = top
                sum_ref[at_rows, :] = total
                high, low = split(e)
                e_ref[0, pl.ds(s0, ROWS), :] = high
                e_ref[1, pl.ds(s0, ROWS), :] = low

            over(0, 4 * rows // ROWS, tile)
            kept_scores = pltpu.make_async_copy(
                s_ref, scores_s.at[layer, d, :, span if chunks > 1 else slice(None)], key_sems.at[per + 2]
            )
            kept_scores.start()
            part = nn((e_ref[0], e_ref[1]), split(val_v[:, cols]))
            kept_scores.wait()
            span_q = slice(4 * rows * d, 4 * rows * (d + 1))
            if chunks > 1:
                acc_ref[span_q, :] += part
                pl.when(chunk == 0)(lambda d=d: between(d))
            else:
                acc_ref[span_q, :] = part
                between(d)
        for copy in out:
            copy.wait()

    if chunks > 1:
        over(0, chunks, one)
    else:
        one(0)


def run_forward(rows3, slot, owned, x, small, table, items_q, items_k, rate, masks, seq_size):
    slab = rows3.shape[2]
    width = x.shape[1]
    thin = width // 2
    rows = x.shape[0]
    zs = seq_size // 2
    frames = seq_size * rows
    dma = pltpu.SemaphoreType.DMA
    smem = pl.BlockSpec(memory_space=pltpu.SMEM)
    block = (rows, width)
    tab = table.shape
    saved = [
        (10,) + block, (2, rows, 4 * width), (seq_size, rows, width), (frames, width), (frames, width),
        (8 * rows, 1), tab, (RIM, width), (RIM, width), (2, 4 * rows, frames),
    ]
    n = CHUNKS
    return pl.pallas_call(
        functools.partial(forward_kernel, zs, frames // KEYS),
        in_specs=[WHOLE, smem, smem] + [WHOLE] * 7,
        out_specs=[FAR, WHOLE] + [FAR] * len(saved),
        out_shape=[shape_of(GROUP * n, 2, zs, 2, slab, thin), shape_of(*block)]
        + [shape_of(L, *s) for s in saved],
        scratch_shapes=[
            vmem(n, 2, 2, slab, thin), vmem(n, 2, 2, slab, thin), vmem(n, 2, slab, thin), vmem(n, 2, slab, thin),
            vmem(4, 4, 2, zs, 2, slab, thin), vmem(*block), vmem(10, *block), vmem(2, rows, 4 * width), vmem(L, *block),
            vmem(KEYS, width), vmem(KEYS, width), vmem(KEYS, width), vmem(*tab), vmem(8 * rows, 1),
            vmem(L, RIM, width), vmem(L, RIM, width),
            vmem(rows + 8, width), vmem(8, 5, rows, rows), vmem(4 * rows, KEYS),
            vmem(2, 4 * rows, KEYS, dtype=jnp.bfloat16), vmem(8 * rows, 1), vmem(8 * rows, 1), vmem(8 * rows, 256),
            dma((n,)), dma((n,)), dma((n,)), dma((n,)), dma((n,)), dma((n, zs)), dma((n, zs)),
            dma((n, 2)), dma((n, 2)), dma((n, 2)), dma((n, 2)), dma((n,)), dma((n,)),
            dma((4,)), dma((6,)), dma((L,)), dma((L, zs, 2)), dma((L, zs, 2)), dma((L,)), dma((L,)),
            dma((L, 2)), dma((L, 2)), dma((KEYS // rows + 3,)),
        ],
        compiler_params=pltpu.CompilerParams(
            collective_id=0, has_side_effects=True, vmem_limit_bytes=LIMIT
        ),
        name="forward",
    )(rows3, slot, owned, x, small, table, items_q, items_k, rate, masks)


HOLD = 4
STAGE = 3
RING = 4
BACK_KEYS = 512


class Scatter:
    def __init__(self, zs, g, out, near, own, ga, gy, gb, gz, mine, sems, free):
        self.zs = zs
        self.seq, self.grp, self.z, self.y, self.x, self.c = places()
        self.g, self.out, self.near, self.own = g, out, near, own
        self.ga, self.gy, self.gb, self.gz, self.mine = ga, gy, gb, gz, mine
        (
            self.own_sem, self.keep_sem, self.n_s, self.n_r, self.a_s, self.a_r, self.b_s, self.b_r,
            self.z_s, self.z_r, self.x_s, self.x_r, self.c_s, self.c_r,
        ) = sems
        self.near_free, self.a_free, self.b_free = free
        self.to_core = {"grp": self.grp + 1 - 2 * self.c}
        self.to_x = {"grp": (self.grp + 2) % 4}
        self.to_y = {"seq": self.z * 2 + 1 - self.y}
        self.place = 2 * self.c + self.x
        self.other = 2 * self.c + 1 - self.x

    def n_copy(self, e):
        return remote(
            self.g.at[CHUNKS - 1 - e, 1 - self.c], self.near.at[e % HOLD], self.n_s.at[e], self.n_r.at[e],
            self.to_core,
        )

    def load(self, e):
        return pltpu.make_async_copy(self.g.at[CHUNKS - 1 - e, self.c], self.own, self.own_sem)

    def a_copies(self, e):
        slot = self.near.at[e % HOLD]
        return [
            remote(
                slot.at[1 - self.x, 0], self.ga.at[e % 2], self.a_s.at[e, 0], self.a_r.at[e, 0], self.to_x
            ),
            remote(
                slot.at[:, 1, :, 1 - self.y], self.gy.at[e % 2], self.a_s.at[e, 1], self.a_r.at[e, 1], self.to_y
            ),
        ]

    def b_copies(self, e):
        slot = self.near.at[e % HOLD]
        return [
            remote(
                slot.at[self.x, 0, :, 1 - self.y], self.gb.at[e % 2, 0], self.b_s.at[e, 0], self.b_r.at[e, 0],
                self.to_y,
            ),
            remote(
                slot.at[1 - self.x, 1, :, self.y], self.gb.at[e % 2, 1], self.b_s.at[e, 1], self.b_r.at[e, 1],
                self.to_x,
            ),
        ]

    def z_copy(self, e, d):
        to = (self.z + d) % self.zs
        return remote(
            self.near.at[e % HOLD, self.x, :, to, self.y], self.gz.at[e, d - 1], self.z_s.at[e, d],
            self.z_r.at[e, d], {"seq": to * 2 + self.y},
        )

    def pair(self, e):
        return pl.ds(CHUNKS - 1 - e, 2)

    def x_any(self, e, place):
        return remote(
            self.mine.at[self.pair(e)], self.out.at[self.pair(e), place], self.x_s.at[e], self.x_r.at[e], self.to_x
        )

    def c_any(self, e, parts):
        return [
            remote(p, q, self.c_s.at[e, i], self.c_r.at[e, i], self.to_core) for i, (p, q) in enumerate(parts)
        ]

    def c_copies(self, e):
        far = self.out.at[self.pair(e), self.other]
        return self.c_any(e, [(self.mine.at[self.pair(e)], self.out.at[self.pair(e), self.place]), (far, far)])

    def c_arrivals(self, e):
        sibling = 2 * (1 - self.c) + self.x
        parts = [self.out.at[self.pair(e), p] for p in (sibling, 2 * (1 - self.c) + 1 - self.x)]
        return self.c_any(e, [(p, p) for p in parts])

    def keep(self, e):
        return pltpu.make_async_copy(
            self.mine.at[self.pair(e)], self.out.at[self.pair(e), self.place], self.keep_sem.at[e]
        )

    def start(self, e):
        @pl.when(e >= HOLD)
        def _():
            pl.semaphore_wait(self.near_free, 1)

        self.n_copy(e).start()

    def signal(self, sem, to):
        pl.semaphore_signal(sem, inc=1, device_id=to, device_id_type=MESH)

    def to_a(self, e):
        self.n_copy(e).wait_recv()
        self.load(e).wait()
        slot = e % HOLD

        def add(i):
            self.near[slot, :, :, i] += self.own[:, :, i]

        over(0, self.zs, add)

        @pl.when(e >= 2)
        def _():
            pl.semaphore_wait(self.a_free.at[0], 1)
            pl.semaphore_wait(self.a_free.at[1], 1)

        for copy in self.a_copies(e):
            copy.start()

    def to_b(self, e):
        for copy in self.a_copies(e):
            copy.wait_recv()
        slot = e % HOLD

        def add(i):
            self.near[slot, self.x, 0, i] += self.ga[e % 2, i]
            for j in range(2):
                self.near[slot, j, 1, i, self.y] += self.gy[e % 2, j, i]

        over(0, self.zs, add)

        @pl.when(e + 2 < CHUNKS)
        def _():
            self.signal(self.a_free.at[0], self.to_x)
            self.signal(self.a_free.at[1], self.to_y)

        @pl.when(e >= 2)
        def _():
            pl.semaphore_wait(self.b_free.at[0], 1)
            pl.semaphore_wait(self.b_free.at[1], 1)

        for copy in self.b_copies(e):
            copy.start()

    def to_z(self, e):
        for copy in self.b_copies(e):
            copy.wait_recv()
        slot = e % HOLD

        def add(i):
            for h in range(2):
                self.near[slot, self.x, h, i, self.y] += self.gb[e % 2, h, i]

        over(0, self.zs, add)

        @pl.when(e + 2 < CHUNKS)
        def _():
            self.signal(self.b_free.at[0], self.to_y)
            self.signal(self.b_free.at[1], self.to_x)

        over(1, self.zs, lambda d: self.z_copy(e, d).start())
        self.mine[CHUNKS - 1 - e] = self.near[slot, self.x, :, self.z, self.y]

    def to_out(self, e, last):
        k = CHUNKS - 1 - e

        def add(d):
            self.z_copy(e, d).wait_recv()
            self.mine[k] += self.gz[e, d - 1]

        over(1, self.zs, add)
        if last:
            self.x_any(e, self.place).start()
            self.keep(e).start()
        for copy in [self.n_copy(e)] + self.a_copies(e) + self.b_copies(e):
            copy.wait_send()
        over(1, self.zs, lambda d: self.z_copy(e, d).wait_send())

        @pl.when(e + HOLD < CHUNKS)
        def _():
            self.signal(self.near_free, self.to_core)

    def to_core_out(self, e):
        self.x_any(e, self.other).wait_recv()
        for copy in self.c_copies(e):
            copy.start()

    def pump(self, t, even):
        def stage(lag, fn, *rest):
            @pl.when((t >= lag) & (t - lag < CHUNKS))
            def _():
                fn(t - lag, *rest)

        stage(0, lambda e: self.load(e).start())
        if not even:
            stage(4, self.to_core_out)
        stage(3, self.to_out, even)
        stage(2, self.to_z)
        stage(1, self.to_b)
        stage(0, self.to_a)

    def finish(self, p):
        e = 2 * p + 1
        for copy in self.c_arrivals(e):
            copy.wait_recv()
        self.keep(e).wait()
        self.x_any(e, self.place).wait_send()
        for copy in self.c_copies(e):
            copy.wait_send()


class Staged:
    def __init__(self, buffer, g, sems, layer):
        self.buffer, self.g, self.sems, self.layer = buffer, g, sems, layer
        self.count, self.open = 0, {}

    def copy(self, number, slot):
        j = number % 4
        return pltpu.make_async_copy(
            self.buffer.at[slot], self.g.at[PER * self.layer + number // 4, j // 2, j % 2], self.sems.at[slot]
        )

    def put(self, number, value):
        slot = self.count % STAGE
        self.count += 1
        for other, place in list(self.open.items()):
            if place == slot:
                self.close(other)
        shape, thin = self.buffer.shape[2:], self.buffer.shape[-1]
        for i in range(2):
            self.buffer[slot, i] = value[:, i * thin : (i + 1) * thin].reshape(shape)
        self.copy(number, slot).start()
        self.open[number] = slot

    def close(self, number):
        self.copy(number, self.open.pop(number)).wait()

    def flush(self, chunk):
        for number in list(self.open):
            if number // 4 == chunk:
                self.close(number)


class Sum:
    def __init__(self, zs, layer, d, from_y, from_z, held, extra, load_sem, y_s, y_r, z_s, z_r):
        self.zs, self.layer, self.d = zs, layer, d
        self.from_y, self.from_z, self.held, self.extra = from_y, from_z, held, extra
        self.sems = (load_sem, y_s, y_r, z_s, z_r)
        seq = lax.axis_index("seq")
        self.z, self.y = seq // 2, seq % 2

    def y_copy(self, to):
        _, y_s, y_r, _, _ = self.sems
        return remote(
            self.d.at[self.layer, to * 2 + 1 - self.y], self.from_y.at[self.layer, to],
            y_s.at[self.layer, to], y_r.at[self.layer, to], {"seq": self.z * 2 + 1 - self.y},
        )

    def z_copy(self, to):
        _, _, _, z_s, z_r = self.sems
        return remote(
            self.held.at[to % RING], self.from_z.at[self.layer, self.z], z_s.at[self.layer, to],
            z_r.at[self.layer, self.z], {"seq": to * 2 + self.y},
        )

    def z_arrival(self, source):
        _, _, _, z_s, z_r = self.sems
        return remote(
            self.held.at[source % RING], self.from_z.at[self.layer, source], z_s.at[self.layer, source],
            z_r.at[self.layer, source], {"seq": source * 2 + self.y},
        )

    def fetch(self, source, to, i):
        return pltpu.make_async_copy(source, to, self.sems[0].at[i])

    def both(self, z, to):
        own = self.fetch(self.d.at[self.layer, z * 2 + self.y], to, 0)
        own.start()
        self.y_copy(z).wait_recv()
        got = self.fetch(self.from_y.at[self.layer, z], self.extra, 1)
        got.start()
        own.wait()
        got.wait()
        to[...] += self.extra[...]

    def start(self, low, high):
        over(low, high, lambda z: self.y_copy(z).start())

    def forward(self, low, high):
        def one(to):
            @pl.when((to >= RING) & (to - RING != self.z))
            def _():
                self.z_copy(to - RING).wait_send()

            @pl.when(to != self.z)
            def _():
                self.both(to, self.held.at[to % RING])
                self.z_copy(to).start()

        over(low, high, one)

    def result(self, out):
        self.both(self.z, out)

        def add(source):
            @pl.when(source != self.z)
            def _():
                self.z_arrival(source).wait_recv()
                got = self.fetch(self.from_z.at[self.layer, source], self.extra, 1)
                got.start()
                got.wait()
                out[...] += self.extra[...]

        over(0, self.zs, add)

    def finish(self):
        over(0, self.zs, lambda z: self.y_copy(z).wait_send())

        def sent(to):
            @pl.when(to != self.z)
            def _():
                self.z_copy(to).wait_send()

        over(max(0, self.zs - RING), self.zs, sent)


def backward_kernel(
    zs, chunks,
    cot_ref, small_all, table_ref, rate_ref, masks_ref, whole,
    rows_s, zz_s, hs_s, k_s, val_s, lse_s, p_s, before_s, after_s, scores_s,
    grad_ref, out, small_out, g, dh_s, from_y, from_z,
    weights, staging, near, own, ga, gy, gb, gz, mine, grad_v, kept, z_v, hs_v, k_v, val_v,
    lse_v, p_v, before_v, after_v, ext, dext, rim_before, rim_after,
    s_ref, dp_ref, dctx_v, delta_v, dq_v, dwin, left_v, right_v, dh_own_v, dh_v, held_v, extra_v,
    ds_all, srecv, szr,
    own_sem, keep_sem, n_s, n_r, a_s, a_r, b_s, b_r, z_s, z_r, x_sm, x_rm, c_s, c_r, near_free, a_free, b_free,
    load_sems, save_sems, stage_sems, rim_s, rim_r, key_sems, sum_load, sy_s, sy_r, sz_s, sz_r,
    t_s, t_r, tz_s, tz_r,
):
    seq = lax.axis_index("seq")
    grp = lax.axis_index("grp")
    count = 2 * zs
    enter_all(seq, grp, zs)
    scatter = Scatter(
        zs, g, out, near, own, ga, gy, gb, gz, mine,
        (own_sem, keep_sem, n_s, n_r, a_s, a_r, b_s, b_r, z_s, z_r, x_sm, x_rm, c_s, c_r),
        (near_free, a_free, b_free),
    )
    rows, width = cot_ref.shape
    half = (KERNEL - 1) // 2
    grad_v[...] = cot_ref[...]
    edges = [
        pltpu.make_async_copy(before_s, before_v, save_sems.at[4]),
        pltpu.make_async_copy(after_s, after_v, save_sems.at[5]),
    ]
    for copy in edges:
        copy.start()
    for copy in edges:
        copy.wait()

    def layer_body(lay, carry):
        layer = L - 1 - lay
        e0 = PER * lay
        small = small_all.at[layer]
        ds_ref = ds_all.at[layer]
        ds_ref[...] = jnp.zeros_like(ds_ref)
        staged = Staged(staging, g, stage_sems, layer)

        class Held:
            def __init__(self):
                self.where, self.waited = {}, set()

            def copy(self, chunk):
                return pltpu.make_async_copy(
                    whole.at[pl.ds(GROUP * (PER * layer + chunk), GROUP)],
                    weights.at[pl.ds(GROUP * self.where[chunk], GROUP)],
                    load_sems.at[self.where[chunk]],
                )

            def begin(self, chunk, place):
                self.where[chunk] = place
                self.copy(chunk).start()

            def get(self, n):
                chunk = n // 4
                if chunk not in self.waited:
                    self.copy(chunk).wait()
                    self.waited.add(chunk)
                return joined(weights[GROUP * self.where[chunk] + n % 4])

        def starts(*numbers):
            for i in numbers:
                scatter.start(e0 + i)

        def early(*numbers):
            pl.when(lay == 0)(lambda: starts(*numbers))

        def late(*numbers):
            pl.when(lay > 0)(lambda: starts(*numbers))

        def pumps(*numbers):
            for i in numbers:
                scatter.pump(e0 + i, i % 2 == 0)

        held = Held()
        pairs = {
            "rows": (rows_s.at[layer], kept), "z": (zz_s.at[layer, 1], z_v), "lse": (lse_s.at[layer], lse_v),
            "p": (p_s.at[layer], p_v), "z1": (zz_s.at[layer, 0], z_v),
        }

        def saved(name):
            source, to = pairs[name]
            return pltpu.make_async_copy(source, to, save_sems.at[list(pairs).index(name) % 4])

        for name in ("rows", "z"):
            saved(name).start()
        held.begin(5, 1)
        held.begin(4, 0)
        held.begin(3, 2)
        for name in ("lse", "p"):
            saved(name).start()
        keys = Keys(chunks, layer, hs_s, k_s, val_s, scores_s, hs_v, k_v, val_v, s_ref, key_sems, rows)
        keys.start(0)
        for d in range(2):
            keys.scores(0, d).start()

        saved("rows").wait()
        saved("z").wait()
        unit, scale = norm(kept[V4])
        grad, dg, dc = norm_back(grad_v[...], unit, scale, small[10:11])
        ds_ref[10:11] = dg
        ds_ref[11:12] = dc

        def second_half():
            staged.flush(5)
            early(0)
            pumps(-1)
            late(0)

        grad = ffn_backward(
            grad, kept[V3], z_v, small, 8, held, 16, staged, 16, ds_ref,
            second_half,
        )
        staged.flush(4)
        early(1)
        grad_v[...] = grad
        saved("z1").start()
        fill_ext(ext, before_v[layer, RIM - half : RIM, :], kept[GLU], after_v[layer, 0:half, :])
        conv_backward(grad, ext, masks_ref[...], small, held.get(PC), staged, PC, dext, ds_ref)
        rims = Rims(
            count, layer, dext.at[0:RIM], dext.at[rows + 2 * half - RIM : rows + 2 * half],
            rim_before, rim_after, rim_s, rim_r,
        )
        rims.start()
        held.begin(2, 0)
        pumps(0)
        late(1)

        saved("lse").wait()
        saved("p").wait()
        rims.wait()
        dq_v[...] = dext[half : half + rows, :]
        dq_v[0:half, :] += rim_before[layer, RIM - half : RIM, :]
        dq_v[rows - half : rows, :] += rim_after[layer, 0:half, :]
        grad = gate_backward(
            dq_v[...], grad_v[...], kept[V2], kept[ZA], kept[ZG], small, held.get(PA), held.get(PG),
            staged, PA, ds_ref,
        )
        grad_v[...] = grad
        halves = split(grad)
        staged.put(PO, tn(split(kept[CTX]), halves))
        dctx = nt(halves, split(held.get(PO)))
        dctx_v[...] = dctx
        staged.flush(3)
        held.begin(0, 2)
        early(2)

        prod = dctx_v[...] * kept[CTX]
        for d in range(2):
            cols = slice(256 * d, 256 * d + 256)
            delta_v[4 * rows * d : 4 * rows * (d + 1), :] = jnp.sum(
                stacked(prod[:, cols]), axis=-1, keepdims=True
            )
        pumps(1)
        late(2)
        total = Sum(
            zs, layer, dh_s, from_y, from_z, held_v, extra_v, sum_load, sy_s, sy_r, sz_s, sz_r
        )

        def between():
            pumps(2)

        attention_backward(
            chunks, layer, keys, held, small, staged, kept.at[Q], lse_v,
            dctx_v, delta_v, s_ref, dp_ref, dq_v, dwin, left_v, right_v, weights.at[4:6], dh_s, key_sems,
            rows, seq, between, total,
        )
        total.forward(0, zs // 2)
        attention_ends(
            held, small, staged, rate_ref, table_ref, kept.at[Q], p_v, dq_v, dwin, left_v, right_v, kept.at[V1], dh_own_v,
            ds_ref, rows,
        )
        held.begin(1, 1)
        staged.flush(2)
        starts(3)
        total.forward(zs // 2, zs)
        pumps(3)
        total.result(dh_v)
        unit, scale = norm(kept[V1])
        back, dg, dc = norm_back(dh_own_v[...] + dh_v[...], unit, scale, small[2:3])
        ds_ref[2:3] = dg
        ds_ref[3:4] = dc
        grad = grad_v[...] + back
        saved("z1").wait()

        def first_half():
            staged.flush(1)
            starts(4)
            pumps(4)

        grad_v[...] = ffn_backward(
            grad, kept[X], z_v, small, 0, held, 0, staged, 0, ds_ref, first_half
        )
        staged.flush(0)
        starts(5)
        rims.finish()
        total.finish()
        return carry

    lax.fori_loop(0, L, layer_body, 0)
    grad_ref[...] = grad_v[...]

    z, y = seq // 2, seq % 2
    devices = (
        {"grp": grp + 1 - 2 * (grp % 2)}, {"grp": (grp + 2) % 4}, {"seq": z * 2 + 1 - y},
    )

    def t_copy(i):
        return remote(ds_all, srecv.at[i], t_s.at[i], t_r.at[i], devices[i])

    for i in range(3):
        t_copy(i).start()
        scatter.pump(CHUNKS - 1 + i, i % 2 == 1)
        t_copy(i).wait()
        ds_all[...] += srecv[i]

    def tz_any(d, block):
        return remote(
            ds_all, szr.at[block], tz_s.at[d], tz_r.at[d], {"seq": ((z + d) % zs) * 2 + y}
        )

    over(1, zs, lambda d: tz_any(d, z).start())
    for t in range(CHUNKS + 2, CHUNKS + 4):
        scatter.pump(t, t % 2 == 0)

    def arrived(d):
        tz_any(d, (z + zs - d) % zs).wait_recv()
        tz_any(d, z).wait_send()

    over(1, zs, arrived)
    szr[z] = ds_all[...]
    small_out[...] = szr[0]

    def add(i):
        small_out[...] += szr[i]

    over(1, zs, add)
    over(0, CHUNKS // 2, scatter.finish)


class Keys:
    def __init__(self, chunks, layer, hs_s, k_s, val_s, scores_s, hs_v, k_v, val_v, s_ref, sems, rows):
        self.chunks, self.layer, self.rows = chunks, layer, rows
        self.hs_s, self.k_s, self.val_s = hs_s, k_s, val_s
        self.hs, self.k, self.val, self.sems = hs_v, k_v, val_v, sems
        self.scores_s, self.s_ref = scores_s, s_ref

    def scores(self, chunk, d):
        span = pl.ds(chunk * BACK_KEYS if isinstance(chunk, int) else pl.multiple_of(chunk * BACK_KEYS, BACK_KEYS), BACK_KEYS)
        return pltpu.make_async_copy(
            self.scores_s.at[self.layer, d, :, span], self.s_ref.at[d],
            self.sems.at[BACK_KEYS // self.rows + 2 + d],
        )

    def any(self, chunk, fn):
        per = BACK_KEYS // self.rows
        span = pl.ds(chunk * BACK_KEYS if isinstance(chunk, int) else pl.multiple_of(chunk * BACK_KEYS, BACK_KEYS), BACK_KEYS)
        fn(pltpu.make_async_copy(self.k_s.at[self.layer, span], self.k, self.sems.at[per]))
        fn(pltpu.make_async_copy(self.val_s.at[self.layer, span], self.val, self.sems.at[per + 1]))

        def one(b):
            fn(
                pltpu.make_async_copy(
                    self.hs_s.at[self.layer, chunk * per + b],
                    self.hs.at[pl.ds(pl.multiple_of(b * self.rows, self.rows), self.rows)],
                    self.sems.at[b],
                )
            )

        over(0, per, one)

    def start(self, chunk):
        self.any(chunk, lambda copy: copy.start())

    def wait(self, chunk):
        self.any(chunk, lambda copy: copy.wait())


def attention_backward(
    chunks, layer, keys, held, small, staged, q_v, lse_v,
    dctx_v, delta_v, s_ref, dp_ref, dq_v, dwin, left_v, right_v, dwkv, dh_s, key_sems,
    rows, own, between, total,
):
    per = BACK_KEYS // rows
    wk, wv = split(held.get(PK)), split(held.get(PV))
    dq_v[...] = jnp.zeros_like(dq_v)
    dwin[...] = jnp.zeros_like(dwin)
    left_v[...] = jnp.zeros_like(left_v)
    right_v[...] = jnp.zeros_like(right_v)
    if chunks > 1:
        for i in range(2):
            dwkv[i] = jnp.zeros(dwkv.shape[1:], F32)

    def quad(d, chunk):
        cols = slice(256 * d, 256 * d + 256)
        tall_q = stacked(q_v[:, cols] + small[21:22, cols])
        tall_c = stacked(dctx_v[:, cols])
        ks = split(keys.k[:, cols])
        dp_ref[...] = nt(split(tall_c), split(keys.val[:, cols]))
        keys.scores(chunk, d).wait()
        blocks = [chunk * per + jt for jt in range(per)]
        before = [jnp.where(block <= own - 2, 1.0, 0.0) for block in blocks]
        after = [jnp.where(block >= own + 2, 1.0, 0.0) for block in blocks]

        def tile(i):
            s0 = pl.multiple_of(i * ROWS, ROWS)
            at_rows = pl.ds(pl.multiple_of(4 * rows * d + s0, ROWS), ROWS)
            p = jnp.exp(s_ref[d, pl.ds(s0, ROWS), :] - lse_v[at_rows, :])
            s_ref[d, pl.ds(s0, ROWS), :] = p
            grad = p * (dp_ref[pl.ds(s0, ROWS), :] - delta_v[at_rows, :]) * 0.125
            dp_ref[pl.ds(s0, ROWS), :] = grad
            left = right = None
            for jt in range(per):
                part = grad[:, jt * rows : (jt + 1) * rows]
                left = part * before[jt] if left is None else left + part * before[jt]
                right = part * after[jt] if right is None else right + part * after[jt]
            left_v[at_rows, :] += jnp.sum(left, axis=-1, keepdims=True)
            right_v[at_rows, :] += jnp.sum(right, axis=-1, keepdims=True)

        over(0, 4 * rows // ROWS, tile)
        for i in range(3):
            block = own - 1 + i - chunk * per

            @pl.when((block >= 0) & (block < per))
            def _():
                lanes = pl.ds(pl.multiple_of(block * rows, rows), rows)
                dwin[d, :, i * rows : (i + 1) * rows] = dp_ref[:, lanes]

        dss = split(dp_ref[...])
        dq_v[:, cols] += unstacked(nn(dss, ks), rows)
        keys.val[:, cols] = nn(split(tall_c.T), split(s_ref[d])).T
        keys.k[:, cols] = nn(split(tall_q.T), dss).T
        if chunks > 1:

            @pl.when(chunk + 1 < chunks)
            def _():
                keys.scores(chunk + 1, d).start()

    def one(chunk):
        keys.wait(chunk)
        quad(0, chunk)
        quad(1, chunk)
        hst = split(keys.hs[...].T)
        dk, dval = split(keys.k[...]), split(keys.val[...])
        keys.hs[...] = nt(dk, wk) + nt(dval, wv)

        def store(b):
            return pltpu.make_async_copy(
                keys.hs.at[pl.ds(pl.multiple_of(b * rows, rows), rows)],
                dh_s.at[layer, chunk * per + b],
                key_sems.at[b],
            )

        over(0, per, lambda b: store(b).start())
        dwk, dwv = nn(hst, dk), nn(hst, dval)
        over(0, per, lambda b: store(b).wait())
        total.start(chunk * (per // 2), (chunk + 1) * (per // 2))
        if chunks > 1:
            thin = dwk.shape[1] // 2
            for i, value in enumerate((dwk, dwv)):
                for j in range(2):
                    dwkv[i, j] += value[:, j * thin : (j + 1) * thin].reshape(dwkv.shape[2:])
        else:
            staged.put(PK, dwk)
            staged.put(PV, dwv)
        if chunks > 1:
            pl.when(chunk + 1 < chunks)(lambda: keys.start(chunk + 1))
        pl.when(chunk == 0)(between)

    if chunks > 1:
        over(0, chunks, one)
        staged.put(PK, joined(dwkv[0]))
        staged.put(PV, joined(dwkv[1]))
    else:
        one(0)


def attention_ends(
    held, small, staged, rate_ref, table_ref, q_v, p_v, dq_v, dwin, left_v, right_v, v1_v, dh_own_v, ds_ref, rows,
):
    lane = lax.broadcasted_iota(jnp.int32, (rows, 128), 1)
    shape = (rows, 3 * rows)
    place = lax.broadcasted_iota(jnp.int32, shape, 1) - lax.broadcasted_iota(jnp.int32, shape, 0) - 65
    rate = rate_ref[...]
    qv = q_v[...] + small[22:23]
    dqu = dq_v[...]
    ds_ref[21:22] = jnp.sum(dqu, axis=0, keepdims=True)
    dtable, dqv = [], []
    for d in range(2):
        cols = slice(256 * d, 256 * d + 256)
        near = []
        for n in range(4):
            whole_window = dwin[d, n * rows : (n + 1) * rows, :]
            window = turned(whole_window)
            back = pltpu.roll(window, 3 * rows - 192, 1, stride=1, stride_axis=0)
            back = turned(back[:, :128])
            span = slice(4 * rows * d + n * rows, 4 * rows * d + (n + 1) * rows)
            left = left_v[span, :] + jnp.sum(
                jnp.where(place < 0, whole_window, 0.0), axis=-1, keepdims=True
            )
            right = right_v[span, :] + jnp.sum(
                jnp.where(place > 127, whole_window, 0.0), axis=-1, keepdims=True
            )
            back = back + jnp.where(lane == 0, left, 0.0)
            back = back + jnp.where(lane == 127, right, 0.0)
            near.append(
                jnp.concatenate(
                    [jnp.where(rate == 2, 0.0, back), jnp.where(rate == 2, back, 0.0)], axis=1
                )
            )
        near = split(jnp.concatenate(near, axis=0))
        dtable.append(tn_long(near, split(stacked(qv[:, cols]))))
        dqv.append(unstacked(nn(near, split(p_v[:, cols])), rows))
    dqv = jnp.concatenate(dqv, axis=1)
    ds_ref[22:23] = jnp.sum(dqv, axis=0, keepdims=True)
    staged.put(PP, tn_long(split(table_ref[...]), split(jnp.concatenate(dtable, axis=1))))
    dq = split(dqu + dqv)
    unit, _ = norm(v1_v[...])
    staged.put(PQ, tn(split(unit * small[2:3] + small[3:4]), dq))
    dh_own_v[...] = nt(dq, split(held.get(PQ)))


def run_backward(cot, small, table, rate, masks, whole, saved, seq_size):
    slab = whole.shape[-2]
    width = cot.shape[1]
    half_width = width // 2
    rows = cot.shape[0]
    zs = seq_size // 2
    frames = seq_size * rows
    chunks = frames // BACK_KEYS
    dma = pltpu.SemaphoreType.DMA
    regular = pltpu.SemaphoreType.REGULAR
    block = (rows, width)
    thin = (zs, 2, slab, half_width)
    square = (2,) + thin
    n = CHUNKS
    stream = (L, seq_size, rows, width)
    half = (L, zs, rows, width)
    return pl.pallas_call(
        functools.partial(backward_kernel, zs, chunks),
        in_specs=[WHOLE] * 5 + [FAR] + [FAR] * len(saved),
        out_specs=[WHOLE, FAR, WHOLE, FAR, FAR, FAR, FAR],
        out_shape=[
            shape_of(*block), shape_of(n, GROUP, 2, slab, half_width), shape_of(L, 24, width),
            shape_of(n, 2, 2, *square), shape_of(*stream), shape_of(*half), shape_of(*half),
        ],
        scratch_shapes=[
            vmem(12, *square), vmem(STAGE, *square), vmem(HOLD, 2, *square), vmem(2, *square),
            vmem(2, *thin), vmem(2, 2, zs, slab, half_width), vmem(2, 2, zs, slab, half_width),
            vmem(n, zs - 1, 2, slab, half_width), vmem(n, 2, slab, half_width),
            vmem(*block), vmem(10, *block), vmem(rows, 4 * width), vmem(BACK_KEYS, width), vmem(BACK_KEYS, width),
            vmem(BACK_KEYS, width), vmem(8 * rows, 1), vmem(*table.shape), vmem(L, RIM, width), vmem(L, RIM, width),
            vmem(rows + 8, width), vmem(rows + 8, width), vmem(L, RIM, width), vmem(L, RIM, width),
            vmem(2, 4 * rows, BACK_KEYS), vmem(4 * rows, BACK_KEYS), vmem(*block), vmem(8 * rows, 1),
            vmem(*block), vmem(2, 4 * rows, 3 * rows), vmem(8 * rows, 1), vmem(8 * rows, 1), vmem(*block),
            vmem(*block), vmem(RING, *block), vmem(*block),
            vmem(L, 24, width), vmem(3, L, 24, width),
            vmem(zs, L, 24, width),
            dma, dma((n,)), dma((n,)), dma((n,)), dma((n, 2)), dma((n, 2)), dma((n, 2)), dma((n, 2)),
            dma((n, zs)), dma((n, zs)), dma((n,)), dma((n,)), dma((n, 2)), dma((n, 2)),
            regular, regular((2,)), regular((2,)),
            dma((3,)), dma((6,)), dma((STAGE,)), dma((L, 2)), dma((L, 2)), dma((BACK_KEYS // rows + 4,)), dma((2,)),
            dma((L, zs)), dma((L, zs)), dma((L, zs)), dma((L, zs)), dma((3,)), dma((3,)), dma((zs,)), dma((zs,)),
        ],
        compiler_params=pltpu.CompilerParams(
            collective_id=1, has_side_effects=True, vmem_limit_bytes=LIMIT
        ),
        name="backward",
    )(cot, small, table, rate, masks, whole, *saved)


def on_device(
    frames_in,
    cotangent,
    lengths,
    rate_flags,
    owner_list,
    master,
    moment_one,
    moment_two,
    average,
    small_params,
    small_moment_one,
    small_moment_two,
    small_average,
):
    local_rows, hidden_width = frames_in.shape[1:]
    seq_size = lax.axis_size("seq")
    me = lax.axis_index("grp")
    slab = hidden_width // seq_size
    stream_rows = local_rows * seq_size
    first_row = lax.axis_index("seq") * local_rows
    half_width = (KERNEL - 1) // 2
    lengths_row = lengths[0]
    flags_row = rate_flags[0]
    own_index = first_row + jnp.arange(local_rows, dtype=jnp.int32)
    own_items, _ = frame_info(own_index, lengths_row, flags_row)
    item_numbers = jnp.arange(lengths_row.shape[0], dtype=jnp.int32)
    rate = 1 + jnp.sum(
        jnp.where(own_items[:, None] == item_numbers[None, :], flags_row[None, :], 0),
        axis=1,
        keepdims=True,
    )
    key_items, _ = frame_info(jnp.arange(stream_rows, dtype=jnp.int32), lengths_row, flags_row)
    rim_index = first_row - half_width + jnp.arange(local_rows + 2 * half_width, dtype=jnp.int32)
    rim_items, _ = frame_info(rim_index, lengths_row, flags_row)
    masks = jnp.stack(
        [
            (rim_items[tap : tap + local_rows] == own_items).astype(jnp.float32)
            for tap in range(KERNEL)
        ],
        axis=1,
    )
    items_q, items_k = own_items[:, None], key_items[None, :]
    table = position_tables(hidden_width)

    places_of = jnp.concatenate([24 * layer + jnp.array(ORDER, jnp.int32) for layer in range(L)])
    slot_of = slot_index(owner_list)[places_of]
    local_slot = slot_of - me * CAP
    owned = ((local_slot >= 0) & (local_slot < CAP)).astype(jnp.int32)
    local_slot = jnp.clip(local_slot, 0, CAP - 1)
    w, values, *saved = run_forward(
        master.reshape(CAP, slab, 2, hidden_width // 2).transpose(0, 2, 1, 3), local_slot, owned.astype(jnp.float32), frames_in[0],
        small_params, table, items_q, items_k, rate, masks, seq_size,
    )
    grad, shares, small_sum = run_backward(
        cotangent[0], small_params, table, rate, masks, w, saved, seq_size
    )[:3]
    small_total = small_sum[:, : small_params.shape[1]]
    here = (
        slot_of[None, :] == (me * CAP + jnp.arange(CAP, dtype=jnp.int32))[:, None]
    ).astype(jnp.int32)
    used = jnp.sum(here, axis=1)
    block_of = jnp.sum(here * jnp.arange(here.shape[1], dtype=jnp.int32)[None, :], axis=1)
    new_master, master_copy, new_one, new_two, new_average = update_slots(
        shares.reshape((-1,) + shares.shape[2:]), block_of, used.astype(jnp.float32)[:, None],
        master, moment_one, moment_two, average,
    )
    new_small, new_small_one, new_small_two = adam_step(
        small_params, small_moment_one, small_moment_two, small_total, RATE_SMALL, 0.0
    )
    new_small_average = AVERAGE_KEEP * small_average + (1.0 - AVERAGE_KEEP) * new_small
    return (
        values[None],
        grad[None],
        new_master,
        master_copy,
        new_one,
        new_two,
        new_average,
        new_small,
        new_small_one,
        new_small_two,
        new_small_average,
    )


def solution(mesh):
    in_specs = (
        P("grp", "seq", None),
        P("grp", "seq", None),
        P("grp", None),
        P("grp", None),
        P(),
        P("grp", "seq"),
        P("grp", "seq"),
        P("grp", "seq"),
        P("grp", "seq"),
        P(),
        P(),
        P(),
        P(),
    )
    out_specs = (
        P("grp", "seq", None),
        P("grp", "seq", None),
        P("grp", "seq"),
        P("grp", "seq"),
        P("grp", "seq"),
        P("grp", "seq"),
        P("grp", "seq"),
        P(),
        P(),
        P(),
        P(),
    )
    return jax.shard_map(
        on_device, mesh=mesh, in_specs=in_specs, out_specs=out_specs, check_vma=False
    )
```

time: 3220 us -> 696 us (0.22)
  waiting for transfers between devices: 1770 us -> 0 us
  local copies, waits for them, and re-layouts: 956 us -> 12.8 us
  Pallas kernels: 0 us -> 672 us
  matrix products: 324 us -> 0 us
  other arithmetic: 81.1 us -> 3.94 us
    reduce_scatter x6 -> x0, waiting for transfers between devices: 954 us -> none  [the longest x1 781 us: on_device(): lax.psum_scatter(block_grads, 'seq', scatter_dimension=1, tiled=True)]
    all_gather x6 -> x0, waiting for transfers between devices: 694 us -> none  [the longest x1 388 us: on_device(): slot_rows = lax.all_gather(columns, 'grp', axis=0, tiled=True)]
    pallas_call x0 -> x3, Pallas kernels: none -> 672 us  [the longest x1 349 us: run_backward(): pl.pallas_call(functools.partial(backward_kernel, zs, chunks), in_specs=[...]
    dot_general x116 -> x0, matrix products: 324 us -> none  [the longest x70 181 us: product(): return jnp.dot(left, right, precision=PRECISION_HIGH)]
    unnamed x833 -> x29, local copies, waits for them, and re-layouts: 176 us -> 4.97 us
    dynamic_update_slice x16 -> x0, local copies, waits for them, and re-layouts: 169 us -> none  [attention_core(): lax.scan(jax.checkpoint(visit), initial, (key_blocks, value_blocks, item_...]
    slice x20 -> x0, local copies, waits for them, and re-layouts: 149 us -> none  [the longest x1 88.1 us: on_device(): blocks[14]]
    concatenate x3 -> x0, local copies, waits for them, and re-layouts: 123 us -> none  [the longest x1 122 us: on_device(): jnp.concatenate(layer_blocks, axis=0).reshape(blocks_all.shape[0], -1)]
  transfers between devices with their start and end apart: 21 -> 0, of which waited for: 13 -> 0; matrix products, arithmetic and copies ran while one was open for 12% -> 0% of each run, Pallas kernels for 0% -> 0%
where the time goes in v1:
time: 696 us; the launch traced here: 690 us
  Pallas kernels  672 us (97%)
  local copies, waits for them, and re-layouts  12.8 us (2%)
    pallas_call x1, Pallas kernels, run_backward(): pl.pallas_call(functools.partial(backward_kernel, zs, chunks), in_specs=[...  349 us
    pallas_call x1, Pallas kernels, run_forward(): pl.pallas_call(functools.partial(forward_kernel, zs, frames // KEYS), in_...  310 us

profile of v1, /device:TPU:0, one launch (start us, length us, event | category | flops | bytes accessed | tf_op | source)
XLA Modules:
  0.0 690.0 jit_solution(4689969294554907236)
XLA Ops:
  0.6 3.0 reshape.176
  3.7 0.0 copy-start.8
  3.7 0.0 copy-start.7
  3.7 0.0 copy-start
  3.7 0.0 copy-start.9
  3.7 0.0 copy-start.10
  3.7 1.6 copy.124
  5.4 0.0 copy-done.8
  5.4 0.2 convert_reduce_fusion
  5.5 0.0 copy-done.7
  5.6 0.8 gather_fusion
  6.3 0.5 subtract_clamp_fusion.slot_ref
  6.9 0.5 fusion.7.owned_ref
  7.4 0.0 copy-done
  7.4 0.7 copy.95.small_all
  8.0 0.0 copy-done.9
  8.1 0.2 reduce-window.4
  8.2 0.1 select_reduce_fusion.3
  8.3 0.7 copy.96.iq_ref
  9.1 0.1 select_reduce_fusion
  9.2 0.6 broadcast_add_fusion
  9.8 0.0 copy-done.10
  9.8 0.1 select_reduce_fusion.2
  9.9 0.7 copy.97.rate_ref
  10.6 0.1 select_reduce_fusion.1
  10.7 0.1 compare_bitcast_fusion
  10.8 0.1 stack.50
  10.9 0.1 copy.94
  11.0 0.6 stack.51.masks_ref
  11.6 310.3 %forward.1 = (f32[48,2,4,2,64,256]{5,4,3,2,1,0:T(8,128)}, f32[128,512]{1,0:T(8,128)}, f32[2,10,128,512]{3,2,1,0:T(8,128)}, f32[2,2,128,2048]{3,2,1,0:T(8,128)}, ...) custom-call(f32[16,2,64,256]{3,2,1,0:T(8,128)} %bitcast.44, ...), custom_call_target="tpu_custom_call" | custom-call | tf_op jit(solution)/shard_map/forward/pallas_call | solution.py:900
  321.9 348.9 %backward.1 = (f32[128,512]{1,0:T(8,128)}, f32[12,4,2,64,256]{4,3,2,1,0:T(8,128)}, f32[2,24,512]{2,1,0:T(8,128)}, f32[12,2,2,2,4,2,64,256]{7,6,5,4,3,2,1,0:T(8,1...) custom-call(f32[128,512]{1,0:T(8,128)} %bitcast.46, ...), custom_call_target="tpu_custom_call" | custom-call | tf_op jit(solution)/shard_map/backward/pallas_call | solution.py:1692
  670.8 0.7 fusion.6
  671.5 0.7 copy.100.used_ref
  672.2 0.0 copy-start.3
  672.2 0.0 copy-start.4
  672.2 0.0 copy-start.5
  672.2 0.0 copy-start.6
  672.2 0.0 copy-start.1
  672.2 13.1 %update_slots.1 = (f32[16,32768]{1,0:T(8,128)}, bf16[16,32768]{1,0:T(8,128)(2,1)}, f32[16,32768]{1,0:T(8,128)}, f32[16,32768]{1,0:T(8,128)}, f32[16,32768]{1,0:T(8,128)}) custom-call(s32[16]{0:T(128)} %get-tuple-element.96.block_ref, f32[16,1]{1,0:T(8,128)} %copy.100.used_ref, f32[48,2,64,256]{3,2,1,0:T(8,128)} %bitcast.45, f32[16,32768]{1,0:T(8,128)} %master_ref.1, ...), custom_call_target="tpu_custom_call" | custom-call | tf_op jit(solution)/shard_map/update_slots/pallas_call | solution.py:135
  685.3 0.0 copy-start.2
  685.3 0.0 copy-done.3
  685.3 0.0 copy-done.4
  685.3 0.0 copy-done.5
  685.3 0.0 copy-done.6
  685.4 0.1 fusion.1
  685.5 0.7 copy.106
  686.2 0.7 copy.107
  686.9 0.7 copy.108
  687.6 0.7 copy.109
  688.3 0.0 copy-done.1
  688.3 0.7 copy.127
  689.1 0.0 copy-done.2
  689.1 0.7 copy.128
  (11 shorter events, 0.1 us)
Async XLA Ops:
  3.7 1.7 copy-start.8
  3.7 1.9 copy-start.7
  3.7 3.7 copy-start
  3.7 4.3 copy-start.9
  3.7 6.0 copy-start.10
  672.2 13.1 %copy-start.3 = (f32[2,24,512]{2,1,0:T(8,128)S(1)}, f32[2,24,512]{2,1,0:T(8,128)}, u32[]{:S(2)}) copy-start(f32[2,24,512]{2,1,0:T(8,128)} %get-tuple-element.50) | copy-start | bytes 294916
  672.2 13.1 %copy-start.4 = (f32[2,23,512]{2,0,1:T(2,128)S(1)}, f32[2,23,512]{2,0,1:T(2,128)}, u32[]{:S(2)}) copy-start(f32[2,23,512]{2,0,1:T(2,128)} %param.28) | copy-start | bytes 282628
  672.2 13.1 %copy-start.5 = (f32[2,23,512]{2,0,1:T(2,128)S(1)}, f32[2,23,512]{2,0,1:T(2,128)}, u32[]{:S(2)}) copy-start(f32[2,23,512]{2,0,1:T(2,128)} %param.26) | copy-start | bytes 282628
  672.2 13.1 %copy-start.6 = (f32[2,23,512]{2,0,1:T(2,128)S(1)}, f32[2,23,512]{2,0,1:T(2,128)}, u32[]{:S(2)}) copy-start(f32[2,23,512]{2,0,1:T(2,128)} %param.27) | copy-start | bytes 282628
  672.2 16.1 %copy-start.1 = (f32[128,512]{1,0:T(8,128)S(1)}, f32[128,512]{1,0:T(8,128)}, u32[]{:S(2)}) copy-start(f32[128,512]{1,0:T(8,128)} %get-tuple-element.31) | copy-start | bytes 786436
  685.3 3.7 copy-start.2

commit v2 on v1

--- a/solution.py
+++ b/solution.py
@@ -428,6 +428,10 @@
     pl.semaphore_wait(barrier, zs + 4)
 
 
+def side(even):
+    return 0 if even else 1
+
+
 def joined(halves):
     size = halves.shape[1] * halves.shape[2] * halves.shape[3]
     return jnp.concatenate([halves[i].reshape(size, halves.shape[-1]) for i in range(2)], axis=1)
@@ -460,62 +464,63 @@
             self.sib.at[k, 1 - self.x], self.face.at[k], self.face_s.at[k], self.face_r.at[k], self.to_x
         )
 
-    def z_any(self, k, d, z):
+    def z_any(self, t, d, even, z):
         return remote(
-            self.own.at[k], self.whole.at[GROUP * k + self.place, :, z, self.y], self.z_s.at[k, d], self.z_r.at[k, d],
+            self.own.at[t // 2, side(even)],
+            self.whole.at[GROUP * (t // 2) + self.place, side(even), z, self.y],
+            self.z_s.at[t, d], self.z_r.at[t, d],
             {"seq": ((self.z + d) % self.zs) * 2 + self.y},
         )
 
-    def z_copy(self, k, d):
-        return self.z_any(k, d, self.z)
-
-    def z_arrival(self, k, d):
-        return self.z_any(k, d, (self.z + self.zs - d) % self.zs)
+    def z_copy(self, t, d, even):
+        return self.z_any(t, d, even, self.z)
+
+    def z_arrival(self, t, d, even):
+        return self.z_any(t, d, even, (self.z + self.zs - d) % self.zs)
 
     def keep(self, k):
         return pltpu.make_async_copy(
             self.own.at[k], self.whole.at[GROUP * k + self.place, :, self.z, self.y], self.local.at[k]
         )
 
-    def two(self, k, parts, s, r):
-        return [
-            remote(part, part, s.at[k, i], r.at[k, i], to) for i, (part, to) in enumerate(parts)
-        ]
-
-    def a_any(self, k, first, second):
-        parts = [(first, self.to_y), (second, self.to_x)]
-        return self.two(k, parts, self.a_s, self.a_r)
-
-    def a_copies(self, k):
-        block = self.whole.at[GROUP * k + self.place]
-        return self.a_any(k, block.at[0, :, self.y], block.at[1, :, self.y])
-
-    def a_arrivals(self, k):
-        return self.a_any(
-            k,
-            self.whole.at[GROUP * k + self.place, 0, :, 1 - self.y],
-            self.whole.at[GROUP * k + self.other, 1, :, self.y],
-        )
-
-    def both(self, k, core):
-        return pl.ds(GROUP * k + 2 * core, 2)
-
-    def b_any(self, k, place, y):
-        parts = [
-            (self.whole.at[GROUP * k + place, 0], self.to_x),
-            (self.whole.at[self.both(k, self.c), 1, :, y], self.to_y),
-        ]
-        return self.two(k, parts, self.b_s, self.b_r)
-
-    def b_copies(self, k):
-        return self.b_any(k, self.place, self.y)
-
-    def b_arrivals(self, k):
-        return self.b_any(k, self.other, 1 - self.y)
-
-    def c_any(self, k, core):
-        part = self.whole.at[self.both(k, core)]
-        return remote(part, part, self.c_s.at[k], self.c_r.at[k], self.to_core)
+    def a_copy(self, t, even):
+        part = self.whole.at[GROUP * (t // 2) + self.place, side(even), :, self.y]
+        return remote(part, part, self.a_s.at[t], self.a_r.at[t], self.to_y if even else self.to_x)
+
+    def a_arrival(self, t, even):
+        first = GROUP * (t // 2)
+        if even:
+            part = self.whole.at[first + self.place, side(even), :, 1 - self.y]
+        else:
+            part = self.whole.at[first + self.other, side(even), :, self.y]
+        return remote(part, part, self.a_s.at[t], self.a_r.at[t], self.to_y if even else self.to_x)
+
+    def both(self, t, core):
+        return pl.ds(GROUP * (t // 2) + 2 * core, 2)
+
+    def b_any(self, t, even, place):
+        if even:
+            part = self.whole.at[GROUP * (t // 2) + place, 0]
+        else:
+            part = self.whole.at[self.both(t, self.c), 1, :, place]
+        to = self.to_x if even else self.to_y
+        return remote(part, part, self.b_s.at[t], self.b_r.at[t], to)
+
+    def b_copy(self, t, even):
+        return self.b_any(t, even, self.place if even else self.y)
+
+    def b_arrival(self, t, even):
+        return self.b_any(t, even, self.other if even else 1 - self.y)
+
+    def c_any(self, t, even, core):
+        part = self.whole.at[self.both(t, core), side(even)]
+        return remote(part, part, self.c_s.at[t], self.c_r.at[t], self.to_core)
+
+    def c_copy(self, t, even):
+        return self.c_any(t, even, self.c)
+
+    def c_arrival(self, t, even):
+        return self.c_any(t, even, 1 - self.c)
 
     def begin(self, k):
         for i in range(2):
@@ -528,54 +533,70 @@
             self.sib[k, i] += self.mine(GROUP * k + 2 * self.c + i)
         self.face_copy(k).start()
 
-    def to_z(self, k):
-        self.face_copy(k).wait_recv()
-        self.own[k] = self.sib[k, self.x] + self.face[k]
-        over(1, self.zs, lambda d: self.z_copy(k, d).start())
-        self.keep(k).start()
-
-    def to_a(self, k):
-        over(1, self.zs, lambda d: self.z_arrival(k, d).wait_recv())
-        self.keep(k).wait()
-        for copy in self.a_copies(k):
-            copy.start()
-
-    def to_b(self, k):
-        for copy in self.a_arrivals(k):
-            copy.wait_recv()
-        for copy in self.b_copies(k):
-            copy.start()
-
-    def to_c(self, k):
-        for copy in self.b_arrivals(k):
-            copy.wait_recv()
-        self.c_any(k, self.c).start()
+    def to_z(self, t, even):
+        if even:
+            k = t // 2
+            self.face_copy(k).wait_recv()
+            self.own[k] = self.sib[k, self.x] + self.face[k]
+            self.keep(k).start()
+        over(1, self.zs, lambda d: self.z_copy(t, d, even).start())
+
+    def to_a(self, t, even):
+        over(1, self.zs, lambda d: self.z_arrival(t, d, even).wait_recv())
+        if even:
+            self.keep(t // 2).wait()
+        self.a_copy(t, even).start()
+
+    def to_b(self, t, even):
+        self.a_arrival(t, even).wait_recv()
+        self.b_copy(t, even).start()
+
+    def to_c(self, t, even):
+        self.b_arrival(t, even).wait_recv()
+        self.c_copy(t, even).start()
 
     def open(self):
         over(0, CHUNKS, self.begin)
-        over(0, 5, self.to_face)
-        over(0, 3, self.to_z)
-
-    def step(self, t):
-        def stage(k, fn):
-            @pl.when((k >= 0) & (k < CHUNKS))
+        over(0, 6, self.to_face)
+        for t in range(4):
+            self.to_z(t, t % 2 == 0)
+
+    def step(self, t, even):
+        steps = 2 * CHUNKS
+
+        @pl.when((t >= 4) & (t - 4 < steps))
+        def _():
+            self.to_c(t - 4, even)
+
+        @pl.when((t >= 2) & (t - 2 < steps))
+        def _():
+            self.to_b(t - 2, even)
+
+        @pl.when(t < steps)
+        def _():
+            self.to_a(t, even)
+
+        if even:
+
+            @pl.when(t // 2 + 6 < CHUNKS)
             def _():
-                fn(k)
-
-        stage(t - 2, self.to_b)
-        stage(t, self.to_a)
-        stage(t - 3, self.to_c)
-        stage(t + 5, self.to_face)
-        stage(t + 3, self.to_z)
+                self.to_face(t // 2 + 6)
+
+        @pl.when(t + 4 < steps)
+        def _():
+            self.to_z(t + 4, even)
 
     def arrived(self, k):
-        self.c_any(k, 1 - self.c).wait_recv()
+        for even in (True, False):
+            self.c_arrival(2 * k + (0 if even else 1), even).wait_recv()
 
     def finish(self, k):
-        self.c_any(k, self.c).wait_send()
-        for copy in self.a_copies(k) + self.b_copies(k):
-            copy.wait_send()
-        over(1, self.zs, lambda d: self.z_copy(k, d).wait_send())
+        for even in (True, False):
+            t = 2 * k + (0 if even else 1)
+            self.c_copy(t, even).wait_send()
+            self.b_copy(t, even).wait_send()
+            self.a_copy(t, even).wait_send()
+            over(1, self.zs, lambda d: self.z_copy(t, d, even).wait_send())
         self.face_copy(k).wait_send()
         self.sib_copy(k).wait_send()
 
@@ -673,8 +694,8 @@
         (local, sib_sm, sib_rm, face_sm, face_rm, z_sm, z_rm, a_sm, a_rm, b_sm, b_rm, c_sm, c_rm),
     )
     gather.open()
-    for t in range(5):
-        gather.step(t)
+    for t in range(8):
+        gather.step(t, t % 2 == 0)
     rows, width = x_ref.shape
     x_v[...] = x_ref[...]
     half = (KERNEL - 1) // 2
@@ -704,7 +725,7 @@
 
         def steps(*numbers):
             for i in numbers:
-                gather.step(PER * layer + i)
+                gather.step(2 * PER * layer + i, i % 2 == 0)
 
         def arrived(*numbers):
             for i in numbers:
@@ -735,7 +756,7 @@
         unit, _ = norm(v1)
         h_v[layer] = unit * small[2:3] + small[3:4]
         share.start()
-        steps(5)
+        steps(8, 9)
         arrived(2)
         q = nn(split(h_v[layer]), split(held.get(PQ)))
         kept[Q] = q
@@ -746,12 +767,12 @@
             cols = slice(256 * d, 256 * d + 256)
             place_bias(qv[:, cols], table[:, cols], rate_ref[...], bias_ref, 4 * d)
         share.forward()
-        steps(6, 7, 8)
+        steps(10, 11, 12, 13)
         arrived(3)
         share.wait()
         attention_forward(
             chunks, count, layer, held, small, hs_s, k_s, val_s, scores_s, e_ref, hs_v, k_v, val_v, kept.at[Q], ik_ref, iq_ref,
-            bias_ref, s_ref, top_ref, sum_ref, acc_ref, key_sems, rows, seq, lambda d: steps(9) if d == 0 else None,
+            bias_ref, s_ref, top_ref, sum_ref, acc_ref, key_sems, rows, seq, lambda d: steps(14, 15) if d == 0 else None,
         )
         lse_v[...] = top_ref[...] + jnp.log(sum_ref[...])
         for d in range(2):
@@ -764,18 +785,21 @@
         kept[ZG] = zg
         kept[GLU] = glu
         rims.start()
-        steps(10)
-        arrived(4, 5)
+        steps(16)
+        arrived(4)
+        steps(17)
         rims.wait()
         fill_ext(ext, before[layer, RIM - half : RIM, :], kept[GLU], after[layer, 0:half, :])
         v3 = conv_forward(kept[V2], ext, masks_ref[...], small, held.get(PC))
         kept[V3] = v3
-        v4 = ffn_forward(v3, small, 8, held, 16, z_v.at[1])
+        arrived(5)
+        v4 = ffn_forward(v3, small, 8, held, 16, z_v.at[1], lambda: steps(18))
         kept[V4] = v4
         unit, _ = norm(v4)
         x_v[...] = unit * small[10:11] + small[11:12]
         for copy in saves(layer):
             copy.start()
+        steps(19)
         rims.finish()
         share.finish()
         return carry
@@ -910,8 +934,8 @@
             vmem(L, RIM, width), vmem(L, RIM, width),
             vmem(rows + 8, width), vmem(8, 5, rows, rows), vmem(4 * rows, KEYS),
             vmem(2, 4 * rows, KEYS, dtype=jnp.bfloat16), vmem(8 * rows, 1), vmem(8 * rows, 1), vmem(8 * rows, 256),
-            dma((n,)), dma((n,)), dma((n,)), dma((n,)), dma((n,)), dma((n, zs)), dma((n, zs)),
-            dma((n, 2)), dma((n, 2)), dma((n, 2)), dma((n, 2)), dma((n,)), dma((n,)),
+            dma((n,)), dma((n,)), dma((n,)), dma((n,)), dma((n,)), dma((2 * n, zs)), dma((2 * n, zs)),
+            dma((2 * n,)), dma((2 * n,)), dma((2 * n,)), dma((2 * n,)), dma((2 * n,)), dma((2 * n,)),
             dma((4,)), dma((6,)), dma((L,)), dma((L, zs, 2)), dma((L, zs, 2)), dma((L,)), dma((L,)),
             dma((L, 2)), dma((L, 2)), dma((KEYS // rows + 3,)),
         ],
@@ -922,18 +946,19 @@
     )(rows3, slot, owned, x, small, table, items_q, items_k, rate, masks)
 
 
-HOLD = 4
+HOLD = 5
+LANDED = 3
 STAGE = 3
 RING = 4
 BACK_KEYS = 512
 
 
 class Scatter:
-    def __init__(self, zs, g, out, near, own, ga, gy, gb, gz, mine, sems, free):
+    def __init__(self, zs, g, out, near, own, ga, gy, gb, gz, gz_v, mine, sems, free):
         self.zs = zs
         self.seq, self.grp, self.z, self.y, self.x, self.c = places()
         self.g, self.out, self.near, self.own = g, out, near, own
-        self.ga, self.gy, self.gb, self.gz, self.mine = ga, gy, gb, gz, mine
+        self.ga, self.gy, self.gb, self.gz, self.gz_v, self.mine = ga, gy, gb, gz, gz_v, mine
         (
             self.own_sem, self.keep_sem, self.n_s, self.n_r, self.a_s, self.a_r, self.b_s, self.b_r,
             self.z_s, self.z_r, self.x_s, self.x_r, self.c_s, self.c_r,
@@ -952,16 +977,16 @@
         )
 
     def load(self, e):
-        return pltpu.make_async_copy(self.g.at[CHUNKS - 1 - e, self.c], self.own, self.own_sem)
+        return pltpu.make_async_copy(self.g.at[CHUNKS - 1 - e, self.c], self.own, self.own_sem.at[0])
 
     def a_copies(self, e):
         slot = self.near.at[e % HOLD]
         return [
             remote(
-                slot.at[1 - self.x, 0], self.ga.at[e % 2], self.a_s.at[e, 0], self.a_r.at[e, 0], self.to_x
+                slot.at[1 - self.x, 0], self.ga.at[e % LANDED], self.a_s.at[e, 0], self.a_r.at[e, 0], self.to_x
             ),
             remote(
-                slot.at[:, 1, :, 1 - self.y], self.gy.at[e % 2], self.a_s.at[e, 1], self.a_r.at[e, 1], self.to_y
+                slot.at[:, 1, :, 1 - self.y], self.gy.at[e % LANDED], self.a_s.at[e, 1], self.a_r.at[e, 1], self.to_y
             ),
         ]
 
@@ -1032,7 +1057,7 @@
 
         over(0, self.zs, add)
 
-        @pl.when(e >= 2)
+        @pl.when(e >= LANDED)
         def _():
             pl.semaphore_wait(self.a_free.at[0], 1)
             pl.semaphore_wait(self.a_free.at[1], 1)
@@ -1046,13 +1071,13 @@
         slot = e % HOLD
 
         def add(i):
-            self.near[slot, self.x, 0, i] += self.ga[e % 2, i]
+            self.near[slot, self.x, 0, i] += self.ga[e % LANDED, i]
             for j in range(2):
-                self.near[slot, j, 1, i, self.y] += self.gy[e % 2, j, i]
+                self.near[slot, j, 1, i, self.y] += self.gy[e % LANDED, j, i]
 
         over(0, self.zs, add)
 
-        @pl.when(e + 2 < CHUNKS)
+        @pl.when(e + LANDED < CHUNKS)
         def _():
             self.signal(self.a_free.at[0], self.to_x)
             self.signal(self.a_free.at[1], self.to_y)
@@ -1087,11 +1112,15 @@
     def to_out(self, e, last):
         k = CHUNKS - 1 - e
 
+        over(1, self.zs, lambda d: self.z_copy(e, d).wait_recv())
+        got = pltpu.make_async_copy(self.gz.at[e], self.gz_v, self.own_sem.at[1])
+        got.start()
+        got.wait()
+
         def add(d):
-            self.z_copy(e, d).wait_recv()
-            self.mine[k] += self.gz[e, d - 1]
-
-        over(1, self.zs, add)
+            self.mine[k] += self.gz_v[d]
+
+        over(0, self.zs - 1, add)
         if last:
             self.x_any(e, self.place).start()
             self.keep(e).start()
@@ -1115,11 +1144,11 @@
                 fn(t - lag, *rest)
 
         stage(0, lambda e: self.load(e).start())
+        stage(2, self.to_b)
+        stage(3, self.to_z)
+        stage(4, self.to_out, not even)
         if not even:
-            stage(4, self.to_core_out)
-        stage(3, self.to_out, even)
-        stage(2, self.to_z)
-        stage(1, self.to_b)
+            stage(6, self.to_core_out)
         stage(0, self.to_a)
 
     def finish(self, p):
@@ -1251,8 +1280,8 @@
     zs, chunks,
     cot_ref, small_all, table_ref, rate_ref, masks_ref, whole,
     rows_s, zz_s, hs_s, k_s, val_s, lse_s, p_s, before_s, after_s, scores_s,
-    grad_ref, out, small_out, g, dh_s, from_y, from_z,
-    weights, staging, near, own, ga, gy, gb, gz, mine, grad_v, kept, z_v, hs_v, k_v, val_v,
+    grad_ref, out, small_out, g, dh_s, from_y, from_z, gz,
+    weights, staging, near, own, ga, gy, gb, gz_v, mine, grad_v, kept, z_v, hs_v, k_v, val_v,
     lse_v, p_v, before_v, after_v, ext, dext, rim_before, rim_after,
     s_ref, dp_ref, dctx_v, delta_v, dq_v, dwin, left_v, right_v, dh_own_v, dh_v, held_v, extra_v,
     ds_all, srecv, szr,
@@ -1265,7 +1294,7 @@
     count = 2 * zs
     enter_all(seq, grp, zs)
     scatter = Scatter(
-        zs, g, out, near, own, ga, gy, gb, gz, mine,
+        zs, g, out, near, own, ga, gy, gb, gz, gz_v, mine,
         (own_sem, keep_sem, n_s, n_r, a_s, a_r, b_s, b_r, z_s, z_r, x_sm, x_rm, c_s, c_r),
         (near_free, a_free, b_free),
     )
@@ -1411,7 +1440,7 @@
         )
 
         def between():
-            pumps(2)
+            pass
 
         attention_backward(
             chunks, layer, keys, held, small, staged, kept.at[Q], lse_v,
@@ -1425,7 +1454,9 @@
         )
         held.begin(1, 1)
         staged.flush(2)
-        starts(3)
+        early(3)
+        pumps(2)
+        late(3)
         total.forward(zs // 2, zs)
         pumps(3)
         total.result(dh_v)
@@ -1473,7 +1504,7 @@
         )
 
     over(1, zs, lambda d: tz_any(d, z).start())
-    for t in range(CHUNKS + 2, CHUNKS + 4):
+    for t in range(CHUNKS + 2, CHUNKS + 6):
         scatter.pump(t, t % 2 == 0)
 
     def arrived(d):
@@ -1692,15 +1723,16 @@
     return pl.pallas_call(
         functools.partial(backward_kernel, zs, chunks),
         in_specs=[WHOLE] * 5 + [FAR] + [FAR] * len(saved),
-        out_specs=[WHOLE, FAR, WHOLE, FAR, FAR, FAR, FAR],
+        out_specs=[WHOLE, FAR, WHOLE, FAR, FAR, FAR, FAR, FAR],
         out_shape=[
             shape_of(*block), shape_of(n, GROUP, 2, slab, half_width), shape_of(L, 24, width),
             shape_of(n, 2, 2, *square), shape_of(*stream), shape_of(*half), shape_of(*half),
+            shape_of(n, zs - 1, 2, slab, half_width),
         ],
         scratch_shapes=[
             vmem(12, *square), vmem(STAGE, *square), vmem(HOLD, 2, *square), vmem(2, *square),
-            vmem(2, *thin), vmem(2, 2, zs, slab, half_width), vmem(2, 2, zs, slab, half_width),
-            vmem(n, zs - 1, 2, slab, half_width), vmem(n, 2, slab, half_width),
+            vmem(LANDED, *thin), vmem(LANDED, 2, zs, slab, half_width), vmem(2, 2, zs, slab, half_width),
+            vmem(zs - 1, 2, slab, half_width), vmem(n, 2, slab, half_width),
             vmem(*block), vmem(10, *block), vmem(rows, 4 * width), vmem(BACK_KEYS, width), vmem(BACK_KEYS, width),
             vmem(BACK_KEYS, width), vmem(8 * rows, 1), vmem(*table.shape), vmem(L, RIM, width), vmem(L, RIM, width),
             vmem(rows + 8, width), vmem(rows + 8, width), vmem(L, RIM, width), vmem(L, RIM, width),
@@ -1709,7 +1741,7 @@
             vmem(*block), vmem(RING, *block), vmem(*block),
             vmem(L, 24, width), vmem(3, L, 24, width),
             vmem(zs, L, 24, width),
-            dma, dma((n,)), dma((n,)), dma((n,)), dma((n, 2)), dma((n, 2)), dma((n, 2)), dma((n, 2)),
+            dma((2,)), dma((n,)), dma((n,)), dma((n,)), dma((n, 2)), dma((n, 2)), dma((n, 2)), dma((n, 2)),
             dma((n, zs)), dma((n, zs)), dma((n,)), dma((n,)), dma((n, 2)), dma((n, 2)),
             regular, regular((2,)), regular((2,)),
             dma((3,)), dma((6,)), dma((STAGE,)), dma((L, 2)), dma((L, 2)), dma((BACK_KEYS // rows + 4,)), dma((2,)),

time: 696 us -> 681 us (0.978)
  Pallas kernels: 672 us -> 652 us
    pallas_call x1, Pallas kernels: 349 us -> 338 us  [run_backward(): pl.pallas_call(functools.partial(backward_kernel, zs, chunks), in_specs=[...]
    pallas_call x1, Pallas kernels: 310 us -> 301 us  [run_forward(): pl.pallas_call(functools.partial(forward_kernel, zs, frames // KEYS), in_...]
where the time goes in v2:
time: 681 us; the launch traced here: 670 us
  Pallas kernels  652 us (96%)
  local copies, waits for them, and re-layouts  12.8 us (2%)
    pallas_call x1, Pallas kernels, run_backward(): pl.pallas_call(functools.partial(backward_kernel, zs, chunks), in_specs=[...  338 us
    pallas_call x1, Pallas kernels, run_forward(): pl.pallas_call(functools.partial(forward_kernel, zs, frames // KEYS), in_...  301 us

profile of v2, /device:TPU:0, one launch (start us, length us, event | category | flops | bytes accessed | tf_op | source)
XLA Modules:
  0.0 670.1 jit_solution(13932390923624526020)
XLA Ops:
  0.6 3.0 reshape.176
  3.7 0.0 copy-start.8
  3.7 0.0 copy-start.7
  3.7 0.0 copy-start
  3.7 0.0 copy-start.9
  3.7 0.0 copy-start.10
  3.7 1.6 copy.124
  5.4 0.0 copy-done.8
  5.4 0.2 convert_reduce_fusion
  5.5 0.0 copy-done.7
  5.6 0.8 gather_fusion
  6.3 0.5 subtract_clamp_fusion.slot_ref
  6.9 0.5 fusion.7.owned_ref
  7.4 0.0 copy-done
  7.4 0.7 copy.95.small_all
  8.0 0.0 copy-done.9
  8.1 0.2 reduce-window.4
  8.2 0.1 select_reduce_fusion.3
  8.3 0.7 copy.96.iq_ref
  9.1 0.1 select_reduce_fusion
  9.2 0.6 broadcast_add_fusion
  9.8 0.0 copy-done.10
  9.8 0.1 select_reduce_fusion.2
  9.9 0.7 copy.97.rate_ref
  10.6 0.1 select_reduce_fusion.1
  10.7 0.1 compare_bitcast_fusion
  10.8 0.1 stack.50
  10.9 0.1 copy.94
  11.0 0.6 stack.51.masks_ref
  11.6 301.0 %forward.1 = (f32[48,2,4,2,64,256]{5,4,3,2,1,0:T(8,128)}, f32[128,512]{1,0:T(8,128)}, f32[2,10,128,512]{3,2,1,0:T(8,128)}, f32[2,2,128,2048]{3,2,1,0:T(8,128)}, ...) custom-call(f32[16,2,64,256]{3,2,1,0:T(8,128)} %bitcast.44, ...), custom_call_target="tpu_custom_call" | custom-call | tf_op jit(solution)/shard_map/forward/pallas_call | solution.py:924
  312.6 338.3 %backward.1 = (f32[128,512]{1,0:T(8,128)}, f32[12,4,2,64,256]{4,3,2,1,0:T(8,128)}, f32[2,24,512]{2,1,0:T(8,128)}, f32[12,2,2,2,4,2,64,256]{7,6,5,4,3,2,1,0:T(8,1...) custom-call(f32[128,512]{1,0:T(8,128)} %bitcast.46, ...), custom_call_target="tpu_custom_call" | custom-call | tf_op jit(solution)/shard_map/backward/pallas_call | solution.py:1723
  651.0 0.7 fusion.6
  651.7 0.7 copy.100.used_ref
  652.4 0.0 copy-start.3
  652.4 0.0 copy-start.4
  652.4 0.0 copy-start.5
  652.4 0.0 copy-start.6
  652.4 0.0 copy-start.1
  652.4 13.1 %update_slots.1 = (f32[16,32768]{1,0:T(8,128)}, bf16[16,32768]{1,0:T(8,128)(2,1)}, f32[16,32768]{1,0:T(8,128)}, f32[16,32768]{1,0:T(8,128)}, f32[16,32768]{1,0:T(8,128)}) custom-call(s32[16]{0:T(128)} %get-tuple-element.96.block_ref, f32[16,1]{1,0:T(8,128)} %copy.100.used_ref, f32[48,2,64,256]{3,2,1,0:T(8,128)} %bitcast.45, f32[16,32768]{1,0:T(8,128)} %master_ref.1, ...), custom_call_target="tpu_custom_call" | custom-call | tf_op jit(solution)/shard_map/update_slots/pallas_call | solution.py:135
  665.5 0.0 copy-start.2
  665.5 0.0 copy-done.3
  665.5 0.0 copy-done.4
  665.5 0.0 copy-done.5
  665.5 0.0 copy-done.6
  665.5 0.1 fusion.1
  665.6 0.7 copy.106
  666.4 0.7 copy.107
  667.1 0.7 copy.108
  667.8 0.7 copy.109
  668.5 0.0 copy-done.1
  668.5 0.7 copy.127
  669.2 0.0 copy-done.2
  669.2 0.7 copy.128
  (11 shorter events, 0.1 us)
Async XLA Ops:
  3.7 1.7 copy-start.8
  3.7 1.9 copy-start.7
  3.7 3.7 copy-start
  3.7 4.3 copy-start.9
  3.7 6.0 copy-start.10
  652.4 13.1 %copy-start.3 = (f32[2,24,512]{2,1,0:T(8,128)S(1)}, f32[2,24,512]{2,1,0:T(8,128)}, u32[]{:S(2)}) copy-start(f32[2,24,512]{2,1,0:T(8,128)} %get-tuple-element.50) | copy-start | bytes 294916
  652.4 13.1 %copy-start.4 = (f32[2,23,512]{2,0,1:T(2,128)S(1)}, f32[2,23,512]{2,0,1:T(2,128)}, u32[]{:S(2)}) copy-start(f32[2,23,512]{2,0,1:T(2,128)} %param.28) | copy-start | bytes 282628
  652.4 13.1 %copy-start.5 = (f32[2,23,512]{2,0,1:T(2,128)S(1)}, f32[2,23,512]{2,0,1:T(2,128)}, u32[]{:S(2)}) copy-start(f32[2,23,512]{2,0,1:T(2,128)} %param.26) | copy-start | bytes 282628
  652.4 13.1 %copy-start.6 = (f32[2,23,512]{2,0,1:T(2,128)S(1)}, f32[2,23,512]{2,0,1:T(2,128)}, u32[]{:S(2)}) copy-start(f32[2,23,512]{2,0,1:T(2,128)} %param.27) | copy-start | bytes 282628
  652.4 16.1 %copy-start.1 = (f32[128,512]{1,0:T(8,128)S(1)}, f32[128,512]{1,0:T(8,128)}, u32[]{:S(2)}) copy-start(f32[128,512]{1,0:T(8,128)} %get-tuple-element.31) | copy-start | bytes 786436
  665.5 3.7 copy-start.2

commit v3 on v2

--- a/solution.py
+++ b/solution.py
@@ -152,6 +152,7 @@
     )(block, used, shares, master, moment_one, moment_two, average)
 
 
+RATE, ITEM = KERNEL, KERNEL + 1
 BF16 = jnp.bfloat16
 F32 = jnp.float32
 ROWS = 32
@@ -375,7 +376,7 @@
     head, part = tile // per, tile % per
     r0 = pl.multiple_of(part * ROWS, ROWS)
     s0 = pl.multiple_of(tile * ROWS, ROWS)
-    iq = items_q[pl.ds(r0, ROWS), :]
+    iq = items_q[pl.ds(r0, ROWS), ITEM : ITEM + 1]
     tiles = []
     keys = s_ref.shape[1]
     for jt in range(keys // rows):
@@ -679,7 +680,7 @@
 
 def forward_kernel(
     zs, chunks,
-    rows_ref, slot_ref, owned_ref, x_ref, small_all, table_ref, iq_ref, ik_ref, rate_ref, masks_ref,
+    rows_ref, slot_ref, owned_ref, x_ref, small_all, table_ref, ik_ref, marks_ref,
     whole, out_ref, rows_s, z_s, hs_s, k_s, val_s, lse_s, p_s, before_s, after_s, scores_s,
     table_w, sib, face, own_w, weights, x_v, kept, z_v, h_v, hs_v, k_v, val_v, p_v, lse_v, before, after, ext, bias_ref, s_ref, e_ref, top_ref, sum_ref, acc_ref,
     local, sib_sm, sib_rm, face_sm, face_rm, z_sm, z_rm, a_sm, a_rm, b_sm, b_rm, c_sm, c_rm,
@@ -694,7 +695,7 @@
         (local, sib_sm, sib_rm, face_sm, face_rm, z_sm, z_rm, a_sm, a_rm, b_sm, b_rm, c_sm, c_rm),
     )
     gather.open()
-    for t in range(8):
+    for t in range(6):
         gather.step(t, t % 2 == 0)
     rows, width = x_ref.shape
     x_v[...] = x_ref[...]
@@ -743,7 +744,9 @@
                 return block(n)
 
         held = Held()
-        arrived(0, 1)
+        arrived(0)
+        steps(6, 7)
+        arrived(1)
 
         @pl.when(layer > 0)
         def _():
@@ -765,13 +768,13 @@
         qv = q + small[22:23]
         for d in range(2):
             cols = slice(256 * d, 256 * d + 256)
-            place_bias(qv[:, cols], table[:, cols], rate_ref[...], bias_ref, 4 * d)
+            place_bias(qv[:, cols], table[:, cols], marks_ref[:, RATE : RATE + 1], bias_ref, 4 * d)
         share.forward()
         steps(10, 11, 12, 13)
         arrived(3)
         share.wait()
         attention_forward(
-            chunks, count, layer, held, small, hs_s, k_s, val_s, scores_s, e_ref, hs_v, k_v, val_v, kept.at[Q], ik_ref, iq_ref,
+            chunks, count, layer, held, small, hs_s, k_s, val_s, scores_s, e_ref, hs_v, k_v, val_v, kept.at[Q], ik_ref, marks_ref,
             bias_ref, s_ref, top_ref, sum_ref, acc_ref, key_sems, rows, seq, lambda d: steps(14, 15) if d == 0 else None,
         )
         lse_v[...] = top_ref[...] + jnp.log(sum_ref[...])
@@ -785,21 +788,19 @@
         kept[ZG] = zg
         kept[GLU] = glu
         rims.start()
-        steps(16)
+        steps(16, 17)
         arrived(4)
-        steps(17)
         rims.wait()
         fill_ext(ext, before[layer, RIM - half : RIM, :], kept[GLU], after[layer, 0:half, :])
-        v3 = conv_forward(kept[V2], ext, masks_ref[...], small, held.get(PC))
+        v3 = conv_forward(kept[V2], ext, marks_ref[...], small, held.get(PC))
         kept[V3] = v3
         arrived(5)
-        v4 = ffn_forward(v3, small, 8, held, 16, z_v.at[1], lambda: steps(18))
+        v4 = ffn_forward(v3, small, 8, held, 16, z_v.at[1])
         kept[V4] = v4
         unit, _ = norm(v4)
         x_v[...] = unit * small[10:11] + small[11:12]
         for copy in saves(layer):
             copy.start()
-        steps(19)
         rims.finish()
         share.finish()
         return carry
@@ -823,7 +824,7 @@
 
 
 def attention_forward(
-    chunks, count, layer, held, small, hs_s, k_s, val_s, scores_s, e_ref, hs_v, k_v, val_v, q_v, ik_ref, iq_ref,
+    chunks, count, layer, held, small, hs_s, k_s, val_s, scores_s, e_ref, hs_v, k_v, val_v, q_v, ik_ref, marks_ref,
     bias_ref, s_ref, top_ref, sum_ref, acc_ref, key_sems, rows, own, between,
 ):
     per = KEYS // rows
@@ -861,7 +862,7 @@
 
             def tile(i):
                 scores, same, s0, _ = tile_scores(
-                    s_ref, bias_ref, iq_ref, items_k, i, 4 * d, own, chunk, rows
+                    s_ref, bias_ref, marks_ref, items_k, i, 4 * d, own, chunk, rows
                 )
                 scores = jnp.where(same, scores, -1e30)
                 at_rows = pl.ds(pl.multiple_of(4 * rows * d + s0, ROWS), ROWS)
@@ -905,7 +906,7 @@
         one(0)
 
 
-def run_forward(rows3, slot, owned, x, small, table, items_q, items_k, rate, masks, seq_size):
+def run_forward(rows3, slot, owned, x, small, table, items_k, marks, seq_size):
     slab = rows3.shape[2]
     width = x.shape[1]
     thin = width // 2
@@ -923,7 +924,7 @@
     n = CHUNKS
     return pl.pallas_call(
         functools.partial(forward_kernel, zs, frames // KEYS),
-        in_specs=[WHOLE, smem, smem] + [WHOLE] * 7,
+        in_specs=[WHOLE, smem, smem] + [WHOLE] * 5,
         out_specs=[FAR, WHOLE] + [FAR] * len(saved),
         out_shape=[shape_of(GROUP * n, 2, zs, 2, slab, thin), shape_of(*block)]
         + [shape_of(L, *s) for s in saved],
@@ -943,7 +944,7 @@
             collective_id=0, has_side_effects=True, vmem_limit_bytes=LIMIT
         ),
         name="forward",
-    )(rows3, slot, owned, x, small, table, items_q, items_k, rate, masks)
+    )(rows3, slot, owned, x, small, table, items_k, marks)
 
 
 HOLD = 5
@@ -1278,7 +1279,7 @@
 
 def backward_kernel(
     zs, chunks,
-    cot_ref, small_all, table_ref, rate_ref, masks_ref, whole,
+    cot_ref, small_all, table_ref, marks_ref, whole,
     rows_s, zz_s, hs_s, k_s, val_s, lse_s, p_s, before_s, after_s, scores_s,
     grad_ref, out, small_out, g, dh_s, from_y, from_z, gz,
     weights, staging, near, own, ga, gy, gb, gz_v, mine, grad_v, kept, z_v, hs_v, k_v, val_v,
@@ -1398,7 +1399,7 @@
         grad_v[...] = grad
         saved("z1").start()
         fill_ext(ext, before_v[layer, RIM - half : RIM, :], kept[GLU], after_v[layer, 0:half, :])
-        conv_backward(grad, ext, masks_ref[...], small, held.get(PC), staged, PC, dext, ds_ref)
+        conv_backward(grad, ext, marks_ref[...], small, held.get(PC), staged, PC, dext, ds_ref)
         rims = Rims(
             count, layer, dext.at[0:RIM], dext.at[rows + 2 * half - RIM : rows + 2 * half],
             rim_before, rim_after, rim_s, rim_r,
@@ -1449,7 +1450,7 @@
         )
         total.forward(0, zs // 2)
         attention_ends(
-            held, small, staged, rate_ref, table_ref, kept.at[Q], p_v, dq_v, dwin, left_v, right_v, kept.at[V1], dh_own_v,
+            held, small, staged, marks_ref, table_ref, kept.at[Q], p_v, dq_v, dwin, left_v, right_v, kept.at[V1], dh_own_v,
             ds_ref, rows,
         )
         held.begin(1, 1)
@@ -1660,12 +1661,12 @@
 
 
 def attention_ends(
-    held, small, staged, rate_ref, table_ref, q_v, p_v, dq_v, dwin, left_v, right_v, v1_v, dh_own_v, ds_ref, rows,
+    held, small, staged, marks_ref, table_ref, q_v, p_v, dq_v, dwin, left_v, right_v, v1_v, dh_own_v, ds_ref, rows,
 ):
     lane = lax.broadcasted_iota(jnp.int32, (rows, 128), 1)
     shape = (rows, 3 * rows)
     place = lax.broadcasted_iota(jnp.int32, shape, 1) - lax.broadcasted_iota(jnp.int32, shape, 0) - 65
-    rate = rate_ref[...]
+    rate = marks_ref[:, RATE : RATE + 1]
     qv = q_v[...] + small[22:23]
     dqu = dq_v[...]
     ds_ref[21:22] = jnp.sum(dqu, axis=0, keepdims=True)
@@ -1704,7 +1705,7 @@
     dh_own_v[...] = nt(dq, split(held.get(PQ)))
 
 
-def run_backward(cot, small, table, rate, masks, whole, saved, seq_size):
+def run_backward(cot, small, table, marks, whole, saved, seq_size):
     slab = whole.shape[-2]
     width = cot.shape[1]
     half_width = width // 2
@@ -1722,7 +1723,7 @@
     half = (L, zs, rows, width)
     return pl.pallas_call(
         functools.partial(backward_kernel, zs, chunks),
-        in_specs=[WHOLE] * 5 + [FAR] + [FAR] * len(saved),
+        in_specs=[WHOLE] * 4 + [FAR] + [FAR] * len(saved),
         out_specs=[WHOLE, FAR, WHOLE, FAR, FAR, FAR, FAR, FAR],
         out_shape=[
             shape_of(*block), shape_of(n, GROUP, 2, slab, half_width), shape_of(L, 24, width),
@@ -1751,7 +1752,7 @@
             collective_id=1, has_side_effects=True, vmem_limit_bytes=LIMIT
         ),
         name="backward",
-    )(cot, small, table, rate, masks, whole, *saved)
+    )(cot, small, table, marks, whole, *saved)
 
 
 def on_device(
@@ -1784,19 +1785,19 @@
     rate = 1 + jnp.sum(
         jnp.where(own_items[:, None] == item_numbers[None, :], flags_row[None, :], 0),
         axis=1,
-        keepdims=True,
     )
     key_items, _ = frame_info(jnp.arange(stream_rows, dtype=jnp.int32), lengths_row, flags_row)
     rim_index = first_row - half_width + jnp.arange(local_rows + 2 * half_width, dtype=jnp.int32)
     rim_items, _ = frame_info(rim_index, lengths_row, flags_row)
-    masks = jnp.stack(
+    marks = jnp.stack(
         [
             (rim_items[tap : tap + local_rows] == own_items).astype(jnp.float32)
             for tap in range(KERNEL)
-        ],
+        ]
+        + [rate.astype(jnp.float32), own_items.astype(jnp.float32)],
         axis=1,
     )
-    items_q, items_k = own_items[:, None], key_items[None, :]
+    items_k = key_items.astype(jnp.float32)[None, :]
     table = position_tables(hidden_width)
 
     places_of = jnp.concatenate([24 * layer + jnp.array(ORDER, jnp.int32) for layer in range(L)])
@@ -1806,10 +1807,10 @@
     local_slot = jnp.clip(local_slot, 0, CAP - 1)
     w, values, *saved = run_forward(
         master.reshape(CAP, slab, 2, hidden_width // 2).transpose(0, 2, 1, 3), local_slot, owned.astype(jnp.float32), frames_in[0],
-        small_params, table, items_q, items_k, rate, masks, seq_size,
+        small_params, table, items_k, marks, seq_size,
     )
     grad, shares, small_sum = run_backward(
-        cotangent[0], small_params, table, rate, masks, w, saved, seq_size
+        cotangent[0], small_params, table, marks, w, saved, seq_size
     )[:3]
     small_total = small_sum[:, : small_params.shape[1]]
     here = (

time: 681 us -> 678 us (level)
  no operation moved by 1% of the time
where the time goes in v3:
time: 678 us; the launch traced here: 669 us
  Pallas kernels  653 us (96%)
  local copies, waits for them, and re-layouts  11.9 us (2%)
    pallas_call x1, Pallas kernels, run_backward(): pl.pallas_call(functools.partial(backward_kernel, zs, chunks), in_specs=[...  340 us
    pallas_call x1, Pallas kernels, run_forward(): pl.pallas_call(functools.partial(forward_kernel, zs, frames // KEYS), in_...  300 us

profile of v3, /device:TPU:0, one launch (start us, length us, event | category | flops | bytes accessed | tf_op | source)
XLA Modules:
  0.0 669.3 jit_solution(1408046343239605676)
XLA Ops:
  0.6 3.0 reshape.189
  3.7 0.0 copy-start.8
  3.7 0.0 copy-start.7
  3.7 0.0 copy-start
  3.7 0.0 copy-start.9
  3.7 0.0 copy-start.10
  3.7 1.6 copy.118
  5.4 0.0 copy-done.8
  5.4 0.2 convert_reduce_fusion
  5.5 0.0 copy-done.7
  5.6 0.8 gather_fusion
  6.3 0.5 subtract_clamp_fusion.slot_ref
  6.9 0.5 fusion.7.owned_ref
  7.4 0.0 copy-done
  7.4 0.7 copy.90.small_all
  8.0 0.0 copy-done.9
  8.0 0.2 reduce-window.4
  8.2 0.1 select_reduce_fusion
  8.3 0.6 add_convert_fusion
  8.9 0.1 select_reduce_fusion.1
  9.0 0.1 select_reduce_fusion.3
  9.1 0.1 fusion.16
  9.2 0.0 copy-done.10
  9.2 0.1 select_reduce_fusion.2
  9.4 0.7 copy.91.marks_ref
  10.1 299.5 %forward.1 = (f32[48,2,4,2,64,256]{5,4,3,2,1,0:T(8,128)}, f32[128,512]{1,0:T(8,128)}, f32[2,10,128,512]{3,2,1,0:T(8,128)}, f32[2,2,128,2048]{3,2,1,0:T(8,128)}, ...) custom-call(f32[16,2,64,256]{3,2,1,0:T(8,128)} %bitcast.44, ...), custom_call_target="tpu_custom_call" | custom-call | tf_op jit(solution)/shard_map/forward/pallas_call | solution.py:925
  309.7 340.3 %backward.1 = (f32[128,512]{1,0:T(8,128)}, f32[12,4,2,64,256]{4,3,2,1,0:T(8,128)}, f32[2,24,512]{2,1,0:T(8,128)}, f32[12,2,2,2,4,2,64,256]{7,6,5,4,3,2,1,0:T(8,1...) custom-call(f32[128,512]{1,0:T(8,128)} %bitcast.46, ...), custom_call_target="tpu_custom_call" | custom-call | tf_op jit(solution)/shard_map/backward/pallas_call | solution.py:1724
  650.0 0.7 fusion.6
  650.7 0.7 copy.94.used_ref
  651.4 0.0 copy-start.3
  651.4 0.0 copy-start.4
  651.4 0.0 copy-start.5
  651.4 0.0 copy-start.6
  651.4 0.0 copy-start.1
  651.4 13.2 %update_slots.1 = (f32[16,32768]{1,0:T(8,128)}, bf16[16,32768]{1,0:T(8,128)(2,1)}, f32[16,32768]{1,0:T(8,128)}, f32[16,32768]{1,0:T(8,128)}, f32[16,32768]{1,0:T(8,128)}) custom-call(s32[16]{0:T(128)} %get-tuple-element.96.block_ref, f32[16,1]{1,0:T(8,128)} %copy.94.used_ref, f32[48,2,64,256]{3,2,1,0:T(8,128)} %bitcast.45, f32[16,32768]{1,0:T(8,128)} %master_ref.1, ...), custom_call_target="tpu_custom_call" | custom-call | tf_op jit(solution)/shard_map/update_slots/pallas_call | solution.py:135
  664.6 0.0 copy-start.2
  664.6 0.0 copy-done.3
  664.6 0.0 copy-done.4
  664.6 0.0 copy-done.5
  664.6 0.0 copy-done.6
  664.6 0.1 fusion.1
  664.8 0.7 copy.100
  665.5 0.7 copy.101
  666.2 0.7 copy.102
  666.9 0.7 copy.103
  667.6 0.0 copy-done.1
  667.6 0.7 copy.121
  668.3 0.0 copy-done.2
  668.3 0.7 copy.122
  (12 shorter events, 0.1 us)
Async XLA Ops:
  3.7 1.7 copy-start.8
  3.7 1.9 copy-start.7
  3.7 3.7 copy-start
  3.7 4.3 copy-start.9
  3.7 5.5 copy-start.10
  651.4 13.2 %copy-start.3 = (f32[2,24,512]{2,1,0:T(8,128)S(1)}, f32[2,24,512]{2,1,0:T(8,128)}, u32[]{:S(2)}) copy-start(f32[2,24,512]{2,1,0:T(8,128)} %get-tuple-element.50) | copy-start | bytes 294916
  651.4 13.2 %copy-start.4 = (f32[2,23,512]{2,0,1:T(2,128)S(1)}, f32[2,23,512]{2,0,1:T(2,128)}, u32[]{:S(2)}) copy-start(f32[2,23,512]{2,0,1:T(2,128)} %param.28) | copy-start | bytes 282628
  651.4 13.2 %copy-start.5 = (f32[2,23,512]{2,0,1:T(2,128)S(1)}, f32[2,23,512]{2,0,1:T(2,128)}, u32[]{:S(2)}) copy-start(f32[2,23,512]{2,0,1:T(2,128)} %param.26) | copy-start | bytes 282628
  651.4 13.2 %copy-start.6 = (f32[2,23,512]{2,0,1:T(2,128)S(1)}, f32[2,23,512]{2,0,1:T(2,128)}, u32[]{:S(2)}) copy-start(f32[2,23,512]{2,0,1:T(2,128)} %param.27) | copy-start | bytes 282628
  651.4 16.2 %copy-start.1 = (f32[128,512]{1,0:T(8,128)S(1)}, f32[128,512]{1,0:T(8,128)}, u32[]{:S(2)}) copy-start(f32[128,512]{1,0:T(8,128)} %get-tuple-element.31) | copy-start | bytes 786436
  664.6 3.7 copy-start.2
